TPU v7x, 256 devices: a whole 4x4x8 slice. The times are simulated.
256 devices in a mesh: rep: 4 (over y), fsdp: 64 (over x, z, core).
Axes of the slice: x: 4, y: 4, z: 8, core: 2. Of those that a mesh axis runs over, the one named last changes fastest.
Arguments:
- gradients: bfloat16 [4, 256, 512, 512], P('rep', None, 'fsdp'), may hold values from -0.3125 to 0.3125
- block_owners: int32 [256, 1], replicated, may hold values from 0 to 63; in each aligned block of 64 rows (0 to 63, 64 to 127, ...) at most 2 rows name the same one
- left_stats: float32 [512, 512, 512], P(('rep', 'fsdp')), as said below
- right_stats: float32 [512, 512, 512], P(('rep', 'fsdp')), as said below
- left_roots: bfloat16 [512, 512, 512], P(('rep', 'fsdp')), as said below
- right_roots: bfloat16 [512, 512, 512], P(('rep', 'fsdp')), as said below
Outputs:
- update: bfloat16 [256, 512, 512], P('rep', 'fsdp')
- left_new: float32 [512, 512, 512], P(('rep', 'fsdp'))
- right_new: float32 [512, 512, 512], P(('rep', 'fsdp'))
Inputs may be any that keep to these rules, and one draw needn't show every extreme that they name: `block_owners`: within each quarter of 64 consecutive blocks no owner appears more than 2 times, and in some quarter some owner appears exactly 2 times. `left_stats`: symmetric blocks with a positive diagonal. `right_stats`: symmetric blocks with a positive diagonal. `left_roots`: symmetric blocks with a positive diagonal. `right_roots`: symmetric blocks with a positive diagonal.
All inputs are finite; a program needn't handle non-finite values.
Results may differ from a plain program's by a relative error of at most 0.018.
Values may be sent and summed in bfloat16 or wider, within the bound.
No kernel may reach another device: no remote copies, remote signals or barrier semaphores. Data moves between devices by JAX's collectives and lax.ppermute only.
A program may use at most 64 MiB of HBM per device.

v0:
```python
import jax
import jax.numpy as jnp
from jax import lax
from jax.sharding import PartitionSpec as P


def slot_places(owner_table, owner_count):
    per_quarter = owner_table.shape[1]
    same_owner = owner_table[:, :, None] == owner_table[:, None, :]
    earlier = lax.broadcasted_iota(jnp.int32, (per_quarter, per_quarter), 1) < lax.broadcasted_iota(
        jnp.int32, (per_quarter, per_quarter), 0
    )
    slot_rank = jnp.sum((same_owner & earlier[None]).astype(jnp.int32), axis=2)
    return slot_rank * owner_count + owner_table


def on_device(gradients, block_owners, left_stats, right_stats, left_roots, right_roots):
    rep_count = lax.axis_size("rep")
    owner_count = lax.axis_size("fsdp")
    slot_count = left_stats.shape[0]
    replica_rows = gradients[0]
    block_count = replica_rows.shape[0]
    row_count = replica_rows.shape[1]
    block_width = replica_rows.shape[2]
    per_quarter = block_count // rep_count
    quarter = lax.axis_index("rep")
    owner_table = block_owners[:, 0].reshape(rep_count, per_quarter)
    placing = slot_places(owner_table, owner_count)
    my_places = lax.dynamic_index_in_dim(placing, quarter, 0, keepdims=False)
    summed = lax.psum_scatter(
        replica_rows.astype(jnp.float32).astype(jnp.bfloat16),
        "rep",
        scatter_dimension=0,
        tiled=True,
    ).astype(jnp.float32)
    buffer = (
        jnp.zeros((slot_count * owner_count, row_count, block_width), jnp.float32)
        .at[my_places]
        .set(summed)
    )
    arrived = lax.all_to_all(
        buffer.reshape(slot_count, owner_count, row_count, block_width).astype(jnp.bfloat16),
        "fsdp",
        split_axis=1,
        concat_axis=1,
        tiled=True,
    ).astype(jnp.float32)
    blocks = arrived.reshape(slot_count, owner_count * row_count, block_width)
    left_new = left_stats + jnp.einsum(
        "sij,skj->sik",
        blocks,
        blocks,
        precision=lax.Precision.HIGHEST,
        preferred_element_type=jnp.float32,
    )
    right_new = right_stats + jnp.einsum(
        "sji,sjk->sik",
        blocks,
        blocks,
        precision=lax.Precision.HIGHEST,
        preferred_element_type=jnp.float32,
    )
    rounded = blocks.astype(jnp.bfloat16)
    left_half = jnp.einsum(
        "sij,sjk->sik", left_roots, rounded, preferred_element_type=jnp.float32
    ).astype(jnp.bfloat16)
    update_slots = jnp.einsum(
        "sij,sjk->sik", left_half, right_roots, preferred_element_type=jnp.float32
    ).astype(jnp.bfloat16)
    returned = lax.all_to_all(
        update_slots.reshape(slot_count, owner_count, row_count, block_width),
        "fsdp",
        split_axis=1,
        concat_axis=1,
        tiled=True,
    )
    update = returned.reshape(slot_count * owner_count, row_count, block_width)[my_places]
    return (update, left_new, right_new)


def solution(mesh):
    placed = (
        P("rep", None, "fsdp", None),
        P(),
        P(("rep", "fsdp"), None, None),
        P(("rep", "fsdp"), None, None),
        P(("rep", "fsdp"), None, None),
        P(("rep", "fsdp"), None, None),
    )
    return jax.shard_map(
        on_device,
        mesh=mesh,
        in_specs=placed,
        out_specs=(
            P("rep", "fsdp", None),
            P(("rep", "fsdp"), None, None),
            P(("rep", "fsdp"), None, None),
        ),
        check_vma=False,
    )
```

profile of v0, /device:TPU:1, one launch (start us, length us, event | category | flops | bytes accessed | tf_op | source)
XLA Modules:
  0.0 141.4 jit_solution(1111449173039111879)
XLA Ops:
  7.2 0.0 copy-start
  7.2 0.0 copy-start.2
  7.2 0.0 reduce-scatter.2.cloned.1.call-start
  7.2 0.7 reduce-scatter.2.cloned.1.call-update
  7.9 0.5 broadcast.31
  8.4 0.0 copy-done.2
  8.4 0.7 reduce.3
  9.1 0.1 eq.15
  9.2 0.2 convert_reduce_fusion
  9.5 37.2 %reduce-scatter.2.cloned.1.call-done = bf16[64,8,512]{2,1,0:T(8,128)(2,1)} async-done(((bf16[256,8,512]{2,1,0:T(8,128)(2,1)}), bf16[64,8,512]{2,1,0:T(8,128)(2,1)}) %reduce-scatter.2.cloned.1.call-update) | async-done | bytes 524304 | tf_op jit(solution)/shard_map/reduce_scatter | solution.py:30
  46.7 2.1 %convert_element_type.27 = f32[64,8,512]{2,1,0:T(8,128)} convert(bf16[64,8,512]{2,1,0:T(8,128)(2,1)} %reduce-scatter.2.cloned.1.call-done) | non-fusion elementwise | flops 262144 | bytes 1572864 | tf_op jit(solution)/shard_map/convert_element_type | solution.py:35
  48.8 0.2 broadcast_in_dim.2
  49.1 6.2 %scatter_fusion = f32[128,8,512]{2,1,0:T(8,128)S(1)} fusion(f32[128,8,512]{2,1,0:T(8,128)S(1)} %broadcast_in_dim.2, s32[64]{0:T(128)S(1)} %fusion.10, f32[64,8,512]{2,1,0:T(8,128)} %convert_element_type.27), kind=kCustom, calls=%fused_computation.1 | custom fusion | bytes 3145984 | tf_op jit(solution)/shard_map/scatter | solution.py:39
  55.3 0.1 convert_element_type.28
  55.5 0.1 copy.25
  55.6 39.0 %all_to_all.10 = bf16[2,64,8,512]{3,2,0,1:T(8,128)(2,1)S(1)} all-to-all(bf16[2,64,8,512]{3,2,0,1:T(8,128)(2,1)S(1)} %copy.25), channel_id=1, replica_groups=mesh['rep'=4,'fsdp'=64] {'fsdp'}, dimensions={1} | all-to-all | bytes 2097152 | tf_op jit(solution)/shard_map/all_to_all | solution.py:41
  94.6 0.0 copy-done
  94.6 2.7 %fusion = bf16[2,64,8,512]{3,2,1,0:T(8,128)(2,1)S(1)} fusion(bf16[2,512,512]{2,1,0:T(8,128)(2,1)S(1)} %copy-done, bf16[2,512,512]{2,1,0:T(8,128)(2,1)} %param.10, bf16[2,64,8,512]{3,2,0,1:T(8,128)(2,1)S(1)} %all_to_all.10), kind=kOutput, calls=%fused_computation.6 | convolution fusion | flops 1074790400 | bytes 4194304 | tf_op jit(solution)/shard_map/sij,sjk->sik/dot_general | solution.py:67
  97.2 1.1 copy.29
  98.4 6.2 %all-to-all-start.1 = ((bf16[2,64,8,512]{3,2,0,1:T(8,128)(2,1)}), bf16[2,64,8,512]{3,2,0,1:T(8,128)(2,1)S(1)}, u32[]{:S(2)}, u32[]{:S(2)}) async-start(bf16[2,64,8,512]{3,2,0,1:T(8,128)(2,1)} %copy.29), calls=%async_computation.2 | async-start | bytes 2097152 | tf_op jit(solution)/shard_map/all_to_all | solution.py:70
  104.6 0.0 copy-start.1
  104.6 3.8 %convolution_add_fusion = f32[2,512,512]{2,1,0:T(8,128)} fusion(f32[2,512,512]{2,1,0:T(8,128)} %param.9, bf16[2,64,8,512]{3,2,0,1:T(8,128)(2,1)S(1)} %all_to_all.10), kind=kOutput, calls=%fused_computation.2 | convolution fusion | flops 537395200 | bytes 5242880 | tf_op jit(solution)/shard_map/sji,sjk->sik/dot_general | solution.py:56
  108.4 0.0 copy-done.1
  108.4 2.1 %convolution_add_fusion.1 = f32[2,512,512]{2,1,0:T(8,128)} fusion(f32[2,512,512]{2,1,0:T(8,128)S(1)} %copy-done.1, bf16[2,64,8,512]{3,2,0,1:T(8,128)(2,1)S(1)} %all_to_all.10), kind=kOutput, calls=%fused_computation.3 | convolution fusion | flops 537395200 | bytes 5242880 | tf_op jit(solution)/shard_map/sij,skj->sik/dot_general | solution.py:49
  110.5 22.6 %all-to-all-done.1 = bf16[2,64,8,512]{3,2,0,1:T(8,128)(2,1)S(1)} async-done(((bf16[2,64,8,512]{3,2,0,1:T(8,128)(2,1)}), bf16[2,64,8,512]{3,2,0,1:T(8,128)(2,1)S(1)}, u32[]{:S(2)}, u32[]{:S(2)}) %all-to-all-start.1) | async-done | bytes 1048608 | tf_op jit(solution)/shard_map/all_to_all | solution.py:70
  133.1 0.1 copy.30
  133.2 1.4 gather_fusion
  (4 shorter events, 0.0 us)
Async XLA Ops:
  7.2 87.4 %copy-start = (bf16[2,512,512]{2,1,0:T(8,128)(2,1)S(1)}, bf16[2,512,512]{2,1,0:T(8,128)(2,1)}, u32[]{:S(2)}) copy-start(bf16[2,512,512]{2,1,0:T(8,128)(2,1)} %param.11) | copy-start | bytes 3145732
  7.2 1.3 copy-start.2
  7.2 39.5 %reduce-scatter.2.cloned.1.call-start = ((), (), s32[]{:S(2)}) async-start(), calls=%async_computation.3 | async-start | bytes 2621440 | tf_op jit(solution)/shard_map/reduce_scatter | solution.py:30
  98.4 34.8 %all-to-all-start.1 = ((bf16[2,64,8,512]{3,2,0,1:T(8,128)(2,1)}), bf16[2,64,8,512]{3,2,0,1:T(8,128)(2,1)S(1)}, u32[]{:S(2)}, u32[]{:S(2)}) async-start(bf16[2,64,8,512]{3,2,0,1:T(8,128)(2,1)} %copy.29), calls=%async_computation.2 | async-start | bytes 2097152 | tf_op jit(solution)/shard_map/all_to_all | solution.py:70
  104.6 3.8 %copy-start.1 = (f32[2,512,512]{2,1,0:T(8,128)S(1)}, f32[2,512,512]{2,1,0:T(8,128)}, u32[]{:S(2)}) copy-start(f32[2,512,512]{2,1,0:T(8,128)} %param.8) | copy-start | bytes 6291460
Sparse Core Ops, SparseCore 0:
  10.6 36.0 reduce-scatter.1
where the time goes:
time: 142 us; the launch traced here: 141 us
  waiting for transfers between devices  60.5 us (43%)
  blocking collectives  39 us (27%)
  between operations  14.1 us (10%)
  local copies, waits for them, and re-layouts  9.81 us (7%)
  matrix products  8.57 us (6%)
  starting transfers between devices  6.23 us (4%)
  other arithmetic  3.2 us (2%)
    all_to_all x1, blocking collectives, on_device(): lax.all_to_all(buffer.reshape(slot_count, owner_count, row_count, block_w...  39 us
    reduce_scatter x1, waiting for transfers between devices, on_device(): lax.psum_scatter(replica_rows.astype(jnp.float32).astype(jnp.bfloat16), '...  37.2 us
    all_to_all x1, waiting for transfers between devices, on_device(): lax.all_to_all(update_slots.reshape(slot_count, owner_count, row_count, b...  22.6 us
    scatter x1, local copies, waits for them, and re-layouts, on_device(): buffer = jnp.zeros((slot_count * owner_count, row_count, block_width), jn...  6.22 us
    all_to_all x1, starting transfers between devices, on_device(): lax.all_to_all(update_slots.reshape(slot_count, owner_count, row_count, b...  6.19 us
    dot_general x1, matrix products, on_device(): jnp.einsum('sji,sjk->sik', blocks, blocks, precision=lax.Precision.HIGHES...  3.82 us
  transfers between devices with their start and end apart: 2, of which 2 were waited for; matrix products, arithmetic and copies ran while one was open for 5% of the time, Pallas kernels for 0%

commit v1 on v0

v1 whole, which is shorter than its diff:
```python
import jax
import jax.numpy as jnp
from jax import lax
from jax.experimental import pallas as pl
from jax.experimental.pallas import tpu as pltpu
from jax.sharding import PartitionSpec as P

MIB = 1024 * 1024
IN_VMEM = pl.BlockSpec(memory_space=pltpu.VMEM)
IN_SMEM = pl.BlockSpec(memory_space=pltpu.SMEM)
ANYWHERE = pl.BlockSpec(memory_space=pl.ANY)


def my_table(block_owners, quarter, per_quarter):
    owners = lax.dynamic_slice(block_owners, (quarter * per_quarter, 0), (per_quarter, 1))
    same_owner = owners == owners.reshape(1, per_quarter)
    earlier = lax.broadcasted_iota(jnp.int32, (per_quarter, per_quarter), 1) < lax.broadcasted_iota(
        jnp.int32, (per_quarter, per_quarter), 0
    )
    rank = jnp.sum((same_owner & earlier).astype(jnp.int32), axis=1)
    return owners[:, 0], rank


def wide(value):
    return value.astype(jnp.float32)


def cut_kernel(starts_ref, rows_ref, *refs):
    outs, sems = refs[:-1], refs[-1]
    copies = []
    for i, out in enumerate(outs):
        copies.append(
            pltpu.make_async_copy(rows_ref.at[pl.ds(starts_ref[i], out.shape[0])], out, sems.at[i])
        )
    for copy in copies:
        copy.start()
    for copy in copies:
        copy.wait()


def cut(rows, starts, counts):
    return pl.pallas_call(
        cut_kernel,
        in_specs=[IN_SMEM, ANYWHERE],
        out_specs=[IN_VMEM] * len(counts),
        out_shape=[jax.ShapeDtypeStruct((count,) + rows.shape[1:], rows.dtype) for count in counts],
        scratch_shapes=[pltpu.SemaphoreType.DMA((len(counts),))],
        compiler_params=pltpu.CompilerParams(vmem_limit_bytes=8 * MIB),
        cost_estimate=pl.CostEstimate(flops=0, bytes_accessed=2 * MIB, transcendentals=0),
    )(jnp.stack(starts), rows)


def add_kernel(a_ref, b_ref, c_ref, d_ref, ab_ref, cd_ref):
    ab_ref[...] = (wide(a_ref[...]) + wide(b_ref[...])).astype(jnp.bfloat16)
    cd_ref[...] = (wide(c_ref[...]) + wide(d_ref[...])).astype(jnp.bfloat16)


def add_pairs(a, b, c, d):
    return pl.pallas_call(
        add_kernel,
        in_specs=[IN_VMEM] * 4,
        out_specs=[IN_VMEM] * 2,
        out_shape=[jax.ShapeDtypeStruct(a.shape, a.dtype)] * 2,
        compiler_params=pltpu.CompilerParams(vmem_limit_bytes=8 * MIB),
        cost_estimate=pl.CostEstimate(flops=2 * a.size, bytes_accessed=2 * MIB, transcendentals=0),
    )(a, b, c, d)


def place_kernel(owner_ref, rank_ref, own_ref, near_a_ref, near_b_ref, far_a_ref, far_b_ref, out_ref):
    out_ref[...] = jnp.zeros_like(out_ref)
    half = near_a_ref.shape[0]

    def step(i, carry):
        for k, near, far in ((i, near_a_ref, far_a_ref), (i + half, near_b_ref, far_b_ref)):
            total = wide(own_ref[k]) + wide(near[i]) + wide(far[i])
            out_ref[owner_ref[k], rank_ref[k]] = total.astype(jnp.bfloat16)
        return carry

    lax.fori_loop(0, half, step, 0, unroll=4)


def place(owners, rank, own, near_a, near_b, far_a, far_b, owner_count, slot_count):
    shape = (owner_count, slot_count) + own.shape[1:]
    return pl.pallas_call(
        place_kernel,
        in_specs=[IN_SMEM] * 2 + [IN_VMEM] * 5,
        out_specs=IN_VMEM,
        out_shape=jax.ShapeDtypeStruct(shape, jnp.bfloat16),
        compiler_params=pltpu.CompilerParams(vmem_limit_bytes=8 * MIB),
        cost_estimate=pl.CostEstimate(flops=2 * own.size, bytes_accessed=3 * MIB, transcendentals=0),
    )(owners, rank, own, near_a, near_b, far_a, far_b)


def product_kernel(held_ref, left_ref, right_ref, update_ref):
    owner_count, slot_count, rows, order = held_ref.shape
    for s in range(slot_count):
        block = wide(held_ref[:, s]).reshape(order, order).astype(jnp.bfloat16)
        half = jnp.dot(left_ref[s], block, preferred_element_type=jnp.float32).astype(jnp.bfloat16)
        full = jnp.dot(half, right_ref[s], preferred_element_type=jnp.float32)
        update_ref[:, s] = full.reshape(owner_count, rows, order).astype(jnp.bfloat16)


def products(held, left_roots, right_roots):
    return pl.pallas_call(
        product_kernel,
        in_specs=[IN_VMEM] * 3,
        out_specs=IN_VMEM,
        out_shape=jax.ShapeDtypeStruct(held.shape, jnp.bfloat16),
        compiler_params=pltpu.CompilerParams(vmem_limit_bytes=16 * MIB),
        cost_estimate=pl.CostEstimate(flops=2**30, bytes_accessed=4 * MIB, transcendentals=0),
    )(held, left_roots, right_roots)


def stats_kernel(held_ref, left_ref, right_ref, left_out, right_out):
    order = held_ref.shape[3]
    block = wide(held_ref[:, 0]).reshape(order, order).astype(jnp.bfloat16)
    left_out[0] = left_ref[0] + lax.dot_general(
        block, block, (((1,), (1,)), ((), ())), preferred_element_type=jnp.float32
    )
    right_out[0] = right_ref[0] + lax.dot_general(
        block, block, (((0,), (0,)), ((), ())), preferred_element_type=jnp.float32
    )


def statistics(held, left_stats, right_stats):
    owner_count, slot_count, rows, order = held.shape
    matrix = pl.BlockSpec((1, order, order), lambda s: (s, 0, 0))
    return pl.pallas_call(
        stats_kernel,
        grid=(slot_count,),
        in_specs=[pl.BlockSpec((owner_count, 1, rows, order), lambda s: (0, s, 0, 0)), matrix, matrix],
        out_specs=[matrix] * 2,
        out_shape=[jax.ShapeDtypeStruct(left_stats.shape, jnp.float32)] * 2,
        compiler_params=pltpu.CompilerParams(vmem_limit_bytes=24 * MIB),
        cost_estimate=pl.CostEstimate(flops=2**30, bytes_accessed=10 * MIB, transcendentals=0),
    )(held, left_stats, right_stats)


def take_kernel(owner_ref, rank_ref, held_ref, out_ref, gathered, sems):
    count = gathered.shape[0]
    parts = sems.shape[0]
    size = count // parts
    copies = []
    for part in range(parts):
        def step(i, carry):
            k = part * size + i
            gathered[k] = held_ref[owner_ref[k], rank_ref[k]]
            return carry

        lax.fori_loop(0, size, step, 0, unroll=8)
        run = pl.ds(part * size, size)
        copies.append(pltpu.make_async_copy(gathered.at[run], out_ref.at[run], sems.at[part]))
        copies[-1].start()
    for copy in copies:
        copy.wait()


def take(owners, rank, held):
    shape = (owners.shape[0],) + held.shape[2:]
    return pl.pallas_call(
        take_kernel,
        in_specs=[IN_SMEM] * 2 + [IN_VMEM],
        out_specs=ANYWHERE,
        out_shape=jax.ShapeDtypeStruct(shape, jnp.bfloat16),
        scratch_shapes=[pltpu.VMEM(shape, jnp.bfloat16), pltpu.SemaphoreType.DMA((4,))],
        compiler_params=pltpu.CompilerParams(vmem_limit_bytes=8 * MIB),
        cost_estimate=pl.CostEstimate(flops=0, bytes_accessed=2 * MIB, transcendentals=0),
    )(owners, rank, held)


def on_device(gradients, block_owners, left_stats, right_stats, left_roots, right_roots):
    rep_count = lax.axis_size("rep")
    owner_count = lax.axis_size("fsdp")
    slot_count = left_stats.shape[0]
    replica_rows = gradients[0]
    per_quarter = replica_rows.shape[0] // rep_count
    half = per_quarter // 2
    quarter = lax.axis_index("rep")

    def swap(value, bit):
        return lax.ppermute(value, "rep", [(i, i ^ bit) for i in range(rep_count)])

    def start(bit, second):
        return (quarter ^ bit) * per_quarter + second * half

    on_a, on_b, end_a, end_b = cut(
        replica_rows, [start(2, 0), start(2, 1), start(1, 0), start(3, 1)], [half] * 4
    )
    on_a, on_b = swap(on_a, 1), swap(on_b, 3)
    near_a, near_b = swap(end_a, 1), swap(end_b, 3)
    own, pass_a, pass_b = cut(
        replica_rows, [start(0, 0), start(3, 0), start(1, 1)], [per_quarter, half, half]
    )
    on_a, on_b = add_pairs(pass_a, on_a, pass_b, on_b)
    far_a, far_b = swap(on_a, 3), swap(on_b, 1)

    owners, rank = my_table(block_owners, quarter, per_quarter)
    placed = place(owners, rank, own, near_a, near_b, far_a, far_b, owner_count, slot_count)
    held = lax.all_to_all(placed, "fsdp", split_axis=0, concat_axis=0, tiled=True)
    update_slots = products(held, left_roots, right_roots)
    returned = lax.all_to_all(update_slots, "fsdp", split_axis=0, concat_axis=0, tiled=True)
    left_new, right_new = statistics(held, left_stats, right_stats)
    update = take(owners, rank, returned)
    return (update, left_new, right_new)


def solution(mesh):
    placed = (
        P("rep", None, "fsdp", None),
        P(),
        P(("rep", "fsdp"), None, None),
        P(("rep", "fsdp"), None, None),
        P(("rep", "fsdp"), None, None),
        P(("rep", "fsdp"), None, None),
    )
    return jax.shard_map(
        on_device,
        mesh=mesh,
        in_specs=placed,
        out_specs=(
            P("rep", "fsdp", None),
            P(("rep", "fsdp"), None, None),
            P(("rep", "fsdp"), None, None),
        ),
        check_vma=False,
    )
```

time: 142 us -> 107 us (0.75)
  waiting for transfers between devices: 60.5 us -> 34.2 us
  between operations: 14.1 us -> 0.72 us
  Pallas kernels: 0 us -> 10.5 us
  matrix products: 8.57 us -> 0 us
  starting transfers between devices: 6.23 us -> 13.6 us
  local copies, waits for them, and re-layouts: 9.81 us -> 4.86 us
  blocking collectives: 39 us -> 42.5 us
  other arithmetic: 3.2 us -> 0.33 us
    reduce_scatter x1 -> x0, waiting for transfers between devices: 37.2 us -> none  [on_device(): lax.psum_scatter(replica_rows.astype(jnp.float32).astype(jnp.bfloat16), '...]
    ppermute x0 -> x6, waiting for transfers between devices: none -> 11.5 us  [swap(): return lax.ppermute(value, 'rep', [(i, i ^ bit) for i in range(rep_count)])]
    pallas_call x0 -> x7, Pallas kernels: none -> 10.5 us  [the longest x1 2.65 us: statistics(): pl.pallas_call(stats_kernel, grid=(slot_count,), in_specs=[pl.BlockSpec((...]
    dot_general x3 -> x0, matrix products: 8.57 us -> none  [the longest x1 3.82 us: on_device(): jnp.einsum('sji,sjk->sik', blocks, blocks, precision=lax.Precision.HIGHES...]
    ppermute x0 -> x6, starting transfers between devices: none -> 7.38 us  [swap(): return lax.ppermute(value, 'rep', [(i, i ^ bit) for i in range(rep_count)])]
    scatter x1 -> x0, local copies, waits for them, and re-layouts: 6.22 us -> none  [on_device(): buffer = jnp.zeros((slot_count * owner_count, row_count, block_width), jn...]
    unnamed x7 -> x14, local copies, waits for them, and re-layouts: 0.53 us -> 4.79 us
    all_to_all x1, blocking collectives: 39 us -> 42.5 us  [on_device(): lax.all_to_all(placed, 'fsdp', split_axis=0, concat_axis=0, tiled=True)]
  transfers between devices with their start and end apart: 2 -> 7, of which waited for: 2 -> 5; matrix products, arithmetic and copies ran while one was open for 5% -> 0% of each run, Pallas kernels for 0% -> 4%
where the time goes in v1:
time: 107 us
  blocking collectives  42.5 us (40%)
  waiting for transfers between devices  34.2 us (32%)
  starting transfers between devices  13.6 us (13%)
  Pallas kernels  10.5 us (10%)
  local copies, waits for them, and re-layouts  4.86 us (5%)
    all_to_all x1, blocking collectives, on_device(): lax.all_to_all(placed, 'fsdp', split_axis=0, concat_axis=0, tiled=True)  42.5 us
    all_to_all x1, waiting for transfers between devices, on_device(): lax.all_to_all(update_slots, 'fsdp', split_axis=0, concat_axis=0, tiled=T...  22.7 us
    ppermute x6, waiting for transfers between devices, swap(): return lax.ppermute(value, 'rep', [(i, i ^ bit) for i in range(rep_count)])  11.5 us
    ppermute x6, starting transfers between devices, swap(): return lax.ppermute(value, 'rep', [(i, i ^ bit) for i in range(rep_count)])  7.38 us
    all_to_all x1, starting transfers between devices, on_device(): lax.all_to_all(update_slots, 'fsdp', split_axis=0, concat_axis=0, tiled=T...  6.19 us
    unnamed x14, local copies, waits for them, and re-layouts  4.79 us
    pallas_call x1, Pallas kernels, statistics(): pl.pallas_call(stats_kernel, grid=(slot_count,), in_specs=[pl.BlockSpec((...  2.65 us
    pallas_call x2, Pallas kernels, cut(): pl.pallas_call(cut_kernel, in_specs=[IN_SMEM, ANYWHERE], out_specs=[IN_VM...  2.27 us
  transfers between devices with their start and end apart: 7, of which 5 were waited for; matrix products, arithmetic and copies ran while one was open for 0% of the time, Pallas kernels for 4%

profile of v1, /device:TPU:1, one launch (start us, length us, event | category | flops | bytes accessed | tf_op | source)
XLA Modules:
  0.0 106.7 jit_solution(16641124663199774679)
XLA Ops:
  0.6 0.0 copy-start
  0.7 0.1 pad_add_fusion.1.starts_ref
  0.7 1.6 %copy-done.1 = bf16[1,256,8,512]{3,2,1,0:T(8,128)(2,1)S(1)} copy-done((bf16[1,256,8,512]{3,2,1,0:T(8,128)(2,1)S(1)}, bf16[1,256,8,512]{3,2,1,0:T(8,128)(2,1)}, u32[]{:S(2)}) %copy-start.1) | copy-done | bytes 2097176
  2.3 1.6 %shard_map.86 = (bf16[32,8,512]{2,1,0:T(8,128)(2,1)}, bf16[32,8,512]{2,1,0:T(8,128)(2,1)}, bf16[32,8,512]{2,1,0:T(8,128)(2,1)}, bf16[32,8,512]{2,1,0:T(8,128)(2,1)}) custom-call(s32[4]{0:T(128)S(1)} %pad_add_fusion.1.starts_ref, bf16[256,8,512]{2,1,0:T(8,128)(2,1)S(1)} %bitcast.10), custom_call_target="tpu_custom_call" | custom-call | bytes 2097152 | tf_op jit(solution)/shard_map/pallas_call | solution.py:42
  4.0 2.2 %collective-permute-start.2 = (bf16[32,8,512]{2,1,0:T(8,128)(2,1)}, bf16[32,8,512]{2,1,0:T(8,128)(2,1)S(1)}, u32[]{:S(2)}, u32[]{:S(2)}) collective-permute-start(bf16[32,8,512]{2,1,0:T(8,128)(2,1)} %get-tuple-element.18), channel_id=1, source_target_pairs={{0,64},{64,0},{128,192},{192,128},{1,65},{65,1},{129,193},{193,129... | collective-permute-start | bytes 786440 | tf_op jit(solution)/shard_map/ppermute | solution.py:181
  6.2 1.9 %collective-permute-start.3 = (bf16[32,8,512]{2,1,0:T(8,128)(2,1)}, bf16[32,8,512]{2,1,0:T(8,128)(2,1)}, u32[]{:S(2)}, u32[]{:S(2)}) collective-permute-start(bf16[32,8,512]{2,1,0:T(8,128)(2,1)} %get-tuple-element.20), channel_id=1, source_target_pairs={{0,192},{64,128},{128,64},{192,0},{1,193},{65,129},{129,65},{193,1... | collective-permute-start | bytes 786440 | tf_op jit(solution)/shard_map/ppermute | solution.py:181
  8.1 0.4 collective-permute-start
  8.5 0.6 collective-permute-start.1
  9.1 0.1 pad_add_fusion.starts_ref
  9.1 0.0 copy-done.2
  9.2 0.7 shard_map.85
  9.8 1.5 %collective-permute-done.2.b_ref = bf16[32,8,512]{2,1,0:T(8,128)(2,1)S(1)} collective-permute-done((bf16[32,8,512]{2,1,0:T(8,128)(2,1)}, bf16[32,8,512]{2,1,0:T(8,128)(2,1)S(1)}, u32[]{:S(2)}, u32[]{:S(2)}) %collective-permute-start.2) | collective-permute-done | bytes 262176 | tf_op jit(solution)/shard_map/ppermute | solution.py:181
  11.3 3.0 %collective-permute-done.3.d_ref = bf16[32,8,512]{2,1,0:T(8,128)(2,1)} collective-permute-done((bf16[32,8,512]{2,1,0:T(8,128)(2,1)}, bf16[32,8,512]{2,1,0:T(8,128)(2,1)}, u32[]{:S(2)}, u32[]{:S(2)}) %collective-permute-start.3) | collective-permute-done | bytes 262176 | tf_op jit(solution)/shard_map/ppermute | solution.py:181
  14.3 1.1 %shard_map.87 = (bf16[32,8,512]{2,1,0:T(8,128)(2,1)S(1)}, bf16[32,8,512]{2,1,0:T(8,128)(2,1)S(1)}) custom-call(bf16[32,8,512]{2,1,0:T(8,128)(2,1)S(1)} %get-tuple-element.17.a_ref, bf16[32,8,512]{2,1,0:T(8,128)(2,1)S(1)} %collective-permute-done.2.b_ref, bf16[32,8,512]{2,1,0:T(8,128)(2,1)S(1)} %get-tuple-element.19.c_ref, ...), custom_call_target="tpu_custom_call" | custom-call | flops 262144 | bytes 2097152 | tf_op jit(solution)/shard_map/pallas_call | solution.py:59
  15.4 2.3 %collective-permute-start.4 = (bf16[32,8,512]{2,1,0:T(8,128)(2,1)S(1)}, bf16[32,8,512]{2,1,0:T(8,128)(2,1)S(1)}, u32[]{:S(2)}, u32[]{:S(2)}) collective-permute-start(bf16[32,8,512]{2,1,0:T(8,128)(2,1)S(1)} %get-tuple-element.21), channel_id=1, source_target_pairs={{0,192},{64,128},{128,64},{192,0},{1,193},{65,129},{129,65},{193,1... | collective-permute-start | bytes 786440 | tf_op jit(solution)/shard_map/ppermute | solution.py:181
  17.6 0.0 collective-permute-start.5
  17.6 0.1 dynamic-slice_bitcast_fusion.owner_ref
  17.7 0.2 convert_reduce_fusion.rank_ref
  17.9 0.0 collective-permute-done.near_a_ref
  17.9 1.9 %collective-permute-done.1.near_b_ref = bf16[32,8,512]{2,1,0:T(8,128)(2,1)S(1)} collective-permute-done((bf16[32,8,512]{2,1,0:T(8,128)(2,1)}, bf16[32,8,512]{2,1,0:T(8,128)(2,1)S(1)}, u32[]{:S(2)}, u32[]{:S(2)}) %collective-permute-start.1) | collective-permute-done | bytes 262176 | tf_op jit(solution)/shard_map/ppermute | solution.py:181
  19.8 5.1 %collective-permute-done.4.far_a_ref = bf16[32,8,512]{2,1,0:T(8,128)(2,1)S(1)} collective-permute-done((bf16[32,8,512]{2,1,0:T(8,128)(2,1)S(1)}, bf16[32,8,512]{2,1,0:T(8,128)(2,1)S(1)}, u32[]{:S(2)}, u32[]{:S(2)}) %collective-permute-start.4) | collective-permute-done | bytes 262176 | tf_op jit(solution)/shard_map/ppermute | solution.py:181
  24.9 0.0 collective-permute-done.5.far_b_ref
  24.9 0.8 shard_map.88
  25.8 42.5 %all_to_all.10.held_ref = bf16[64,2,8,512]{3,2,1,0:T(8,128)(2,1)S(1)} all-to-all(bf16[64,2,8,512]{3,2,1,0:T(8,128)(2,1)S(1)} %shard_map.88), channel_id=1, replica_groups=mesh['rep'=4,'fsdp'=64] {'fsdp'}, dimensions={0} | all-to-all | bytes 2097152 | tf_op jit(solution)/shard_map/all_to_all | solution.py:199
  68.3 2.2 %shard_map.89 = bf16[64,2,8,512]{3,2,1,0:T(8,128)(2,1)} custom-call(bf16[64,2,8,512]{3,2,1,0:T(8,128)(2,1)S(1)} %all_to_all.10.held_ref, bf16[2,512,512]{2,1,0:T(8,128)(2,1)S(1)} %copy-done.5, bf16[2,512,512]{2,1,0:T(8,128)(2,1)S(1)} %copy-done.6), custom_call_target="tpu_custom_call" | custom-call | flops 1073741824 | bytes 4194304 | tf_op jit(solution)/shard_map/pallas_call | solution.py:104
  70.5 6.2 %all-to-all-start.1 = ((bf16[64,2,8,512]{3,2,1,0:T(8,128)(2,1)}), bf16[64,2,8,512]{3,2,1,0:T(8,128)(2,1)S(1)}, u32[]{:S(2)}, u32[]{:S(2)}) async-start(bf16[64,2,8,512]{3,2,1,0:T(8,128)(2,1)} %shard_map.89), calls=%async_computation.1 | async-start | bytes 2097152 | tf_op jit(solution)/shard_map/all_to_all | solution.py:201
  76.7 0.0 copy-start.3
  76.7 1.6 %copy-done.3 = f32[2,512,512]{2,1,0:T(8,128)S(1)} copy-done((f32[2,512,512]{2,1,0:T(8,128)S(1)}, f32[2,512,512]{2,1,0:T(8,128)}, u32[]{:S(2)}) %copy-start.3) | copy-done | bytes 2097176
  78.3 1.6 %copy-done.4 = f32[2,512,512]{2,1,0:T(8,128)S(1)} copy-done((f32[2,512,512]{2,1,0:T(8,128)S(1)}, f32[2,512,512]{2,1,0:T(8,128)}, u32[]{:S(2)}) %copy-start.4) | copy-done | bytes 2097176
  79.9 2.6 %shard_map.91 = (f32[2,512,512]{2,1,0:T(8,128)}, f32[2,512,512]{2,1,0:T(8,128)}) custom-call(bf16[64,2,8,512]{3,2,1,0:T(8,128)(2,1)S(1)} %all_to_all.10.held_ref, f32[2,512,512]{2,1,0:T(8,128)S(1)} %copy-done.3, f32[2,512,512]{2,1,0:T(8,128)S(1)} %copy-done.4), custom_call_target="tpu_custom_call" | custom-call | flops 1073741824 | bytes 10485760 | tf_op jit(solution)/shard_map/pallas_call | solution.py:128
  82.6 22.7 %all-to-all-done.1.held_ref = bf16[64,2,8,512]{3,2,1,0:T(8,128)(2,1)S(1)} async-done(((bf16[64,2,8,512]{3,2,1,0:T(8,128)(2,1)}), bf16[64,2,8,512]{3,2,1,0:T(8,128)(2,1)S(1)}, u32[]{:S(2)}, u32[]{:S(2)}) %all-to-all-start.1) | async-done | bytes 1048608 | tf_op jit(solution)/shard_map/all_to_all | solution.py:201
  105.3 1.4 %shard_map.90 = bf16[64,8,512]{2,1,0:T(8,128)(2,1)} custom-call(s32[64]{0:T(128)S(1)} %dynamic-slice_bitcast_fusion.owner_ref, s32[64]{0:T(128)S(1)} %convert_reduce_fusion.rank_ref, bf16[64,2,8,512]{3,2,1,0:T(8,128)(2,1)S(1)} %all-to-all-done.1.held_ref), custom_call_target="tpu_custom_call" | custom-call | bytes 2097152 | tf_op jit(solution)/shard_map/pallas_call | solution.py:160
  (8 shorter events, 0.0 us)
Async XLA Ops:
  0.6 17.0 %copy-start = (s32[256,1]{0,1:T(1,128)S(1)}, s32[256,1]{0,1:T(1,128)}, u32[]{:S(2)}) copy-start(s32[256,1]{0,1:T(1,128)} %param.7) | copy-start | bytes 3076
  0.7 1.6 %copy-start.1 = (bf16[1,256,8,512]{3,2,1,0:T(8,128)(2,1)S(1)}, bf16[1,256,8,512]{3,2,1,0:T(8,128)(2,1)}, u32[]{:S(2)}) copy-start(bf16[1,256,8,512]{3,2,1,0:T(8,128)(2,1)} %param.6) | copy-start | bytes 6291460
  2.3 6.8 %copy-start.2 = (bf16[1,256,8,512]{3,2,1,0:T(8,128)(2,1)S(1)}, bf16[1,256,8,512]{3,2,1,0:T(8,128)(2,1)}, u32[]{:S(2)}) copy-start(bf16[1,256,8,512]{3,2,1,0:T(8,128)(2,1)} %param.6) | copy-start | bytes 6291460
  4.0 7.3 %collective-permute-start.2 = (bf16[32,8,512]{2,1,0:T(8,128)(2,1)}, bf16[32,8,512]{2,1,0:T(8,128)(2,1)S(1)}, u32[]{:S(2)}, u32[]{:S(2)}) collective-permute-start(bf16[32,8,512]{2,1,0:T(8,128)(2,1)} %get-tuple-element.18), channel_id=1, source_target_pairs={{0,64},{64,0},{128,192},{192,128},{1,65},{65,1},{129,193},{193,129... | collective-permute-start | bytes 786440 | tf_op jit(solution)/shard_map/ppermute | solution.py:181
  6.2 8.1 %collective-permute-start.3 = (bf16[32,8,512]{2,1,0:T(8,128)(2,1)}, bf16[32,8,512]{2,1,0:T(8,128)(2,1)}, u32[]{:S(2)}, u32[]{:S(2)}) collective-permute-start(bf16[32,8,512]{2,1,0:T(8,128)(2,1)} %get-tuple-element.20), channel_id=1, source_target_pairs={{0,192},{64,128},{128,64},{192,0},{1,193},{65,129},{129,65},{193,1... | collective-permute-start | bytes 786440 | tf_op jit(solution)/shard_map/ppermute | solution.py:181
  8.1 9.8 %collective-permute-start = (bf16[32,8,512]{2,1,0:T(8,128)(2,1)}, bf16[32,8,512]{2,1,0:T(8,128)(2,1)S(1)}, u32[]{:S(2)}, u32[]{:S(2)}) collective-permute-start(bf16[32,8,512]{2,1,0:T(8,128)(2,1)} %get-tuple-element.15), channel_id=1, source_target_pairs={{0,64},{64,0},{128,192},{192,128},{1,65},{65,1},{129,193},{193,129... | collective-permute-start | bytes 786440 | tf_op jit(solution)/shard_map/ppermute | solution.py:181
  8.5 11.3 %collective-permute-start.1 = (bf16[32,8,512]{2,1,0:T(8,128)(2,1)}, bf16[32,8,512]{2,1,0:T(8,128)(2,1)S(1)}, u32[]{:S(2)}, u32[]{:S(2)}) collective-permute-start(bf16[32,8,512]{2,1,0:T(8,128)(2,1)} %get-tuple-element.16), channel_id=1, source_target_pairs={{0,192},{64,128},{128,64},{192,0},{1,193},{65,129},{129,65},{193,1... | collective-permute-start | bytes 786440 | tf_op jit(solution)/shard_map/ppermute | solution.py:181
  15.4 9.6 %collective-permute-start.4 = (bf16[32,8,512]{2,1,0:T(8,128)(2,1)S(1)}, bf16[32,8,512]{2,1,0:T(8,128)(2,1)S(1)}, u32[]{:S(2)}, u32[]{:S(2)}) collective-permute-start(bf16[32,8,512]{2,1,0:T(8,128)(2,1)S(1)} %get-tuple-element.21), channel_id=1, source_target_pairs={{0,192},{64,128},{128,64},{192,0},{1,193},{65,129},{129,65},{193,1... | collective-permute-start | bytes 786440 | tf_op jit(solution)/shard_map/ppermute | solution.py:181
  17.6 7.3 %collective-permute-start.5 = (bf16[32,8,512]{2,1,0:T(8,128)(2,1)S(1)}, bf16[32,8,512]{2,1,0:T(8,128)(2,1)S(1)}, u32[]{:S(2)}, u32[]{:S(2)}) collective-permute-start(bf16[32,8,512]{2,1,0:T(8,128)(2,1)S(1)} %get-tuple-element.22), channel_id=1, source_target_pairs={{0,64},{64,0},{128,192},{192,128},{1,65},{65,1},{129,193},{193,129... | collective-permute-start | bytes 786440 | tf_op jit(solution)/shard_map/ppermute | solution.py:181
  24.9 43.4 %copy-start.5 = (bf16[2,512,512]{2,1,0:T(8,128)(2,1)S(1)}, bf16[2,512,512]{2,1,0:T(8,128)(2,1)}, u32[]{:S(2)}) copy-start(bf16[2,512,512]{2,1,0:T(8,128)(2,1)} %left_ref.2) | copy-start | bytes 3145732
  24.9 43.4 %copy-start.6 = (bf16[2,512,512]{2,1,0:T(8,128)(2,1)S(1)}, bf16[2,512,512]{2,1,0:T(8,128)(2,1)}, u32[]{:S(2)}) copy-start(bf16[2,512,512]{2,1,0:T(8,128)(2,1)} %right_ref.2) | copy-start | bytes 3145732
  70.5 34.8 %all-to-all-start.1 = ((bf16[64,2,8,512]{3,2,1,0:T(8,128)(2,1)}), bf16[64,2,8,512]{3,2,1,0:T(8,128)(2,1)S(1)}, u32[]{:S(2)}, u32[]{:S(2)}) async-start(bf16[64,2,8,512]{3,2,1,0:T(8,128)(2,1)} %shard_map.89), calls=%async_computation.1 | async-start | bytes 2097152 | tf_op jit(solution)/shard_map/all_to_all | solution.py:201
  76.7 1.6 %copy-start.3 = (f32[2,512,512]{2,1,0:T(8,128)S(1)}, f32[2,512,512]{2,1,0:T(8,128)}, u32[]{:S(2)}) copy-start(f32[2,512,512]{2,1,0:T(8,128)} %left_ref.3) | copy-start | bytes 6291460
  78.3 1.6 %copy-start.4 = (f32[2,512,512]{2,1,0:T(8,128)S(1)}, f32[2,512,512]{2,1,0:T(8,128)}, u32[]{:S(2)}) copy-start(f32[2,512,512]{2,1,0:T(8,128)} %right_ref.3) | copy-start | bytes 6291460

commit v2 on v1

--- a/solution.py
+++ b/solution.py
@@ -9,6 +9,7 @@
 IN_VMEM = pl.BlockSpec(memory_space=pltpu.VMEM)
 IN_SMEM = pl.BlockSpec(memory_space=pltpu.SMEM)
 ANYWHERE = pl.BlockSpec(memory_space=pl.ANY)
+IN_HBM = pl.BlockSpec(memory_space=pltpu.HBM)
 
 
 def my_table(block_owners, quarter, per_quarter):
@@ -41,29 +42,28 @@
 def cut(rows, starts, counts):
     return pl.pallas_call(
         cut_kernel,
-        in_specs=[IN_SMEM, ANYWHERE],
+        in_specs=[IN_SMEM, IN_HBM],
         out_specs=[IN_VMEM] * len(counts),
-        out_shape=[jax.ShapeDtypeStruct((count,) + rows.shape[1:], rows.dtype) for count in counts],
+        out_shape=[pltpu.VMEM((count,) + rows.shape[1:], rows.dtype) for count in counts],
         scratch_shapes=[pltpu.SemaphoreType.DMA((len(counts),))],
         compiler_params=pltpu.CompilerParams(vmem_limit_bytes=8 * MIB),
         cost_estimate=pl.CostEstimate(flops=0, bytes_accessed=2 * MIB, transcendentals=0),
-    )(jnp.stack(starts), rows)
-
-
-def add_kernel(a_ref, b_ref, c_ref, d_ref, ab_ref, cd_ref):
-    ab_ref[...] = (wide(a_ref[...]) + wide(b_ref[...])).astype(jnp.bfloat16)
-    cd_ref[...] = (wide(c_ref[...]) + wide(d_ref[...])).astype(jnp.bfloat16)
-
-
-def add_pairs(a, b, c, d):
+    )(jnp.stack(starts), pltpu.with_memory_space_constraint(rows, pltpu.HBM))
+
+
+def add_kernel(a_ref, b_ref, sum_ref):
+    sum_ref[...] = (wide(a_ref[...]) + wide(b_ref[...])).astype(jnp.bfloat16)
+
+
+def add(a, b):
     return pl.pallas_call(
         add_kernel,
-        in_specs=[IN_VMEM] * 4,
-        out_specs=[IN_VMEM] * 2,
-        out_shape=[jax.ShapeDtypeStruct(a.shape, a.dtype)] * 2,
-        compiler_params=pltpu.CompilerParams(vmem_limit_bytes=8 * MIB),
-        cost_estimate=pl.CostEstimate(flops=2 * a.size, bytes_accessed=2 * MIB, transcendentals=0),
-    )(a, b, c, d)
+        in_specs=[IN_VMEM] * 2,
+        out_specs=IN_VMEM,
+        out_shape=jax.ShapeDtypeStruct(a.shape, a.dtype),
+        compiler_params=pltpu.CompilerParams(vmem_limit_bytes=8 * MIB),
+        cost_estimate=pl.CostEstimate(flops=a.size, bytes_accessed=MIB, transcendentals=0),
+    )(a, b)
 
 
 def place_kernel(owner_ref, rank_ref, own_ref, near_a_ref, near_b_ref, far_a_ref, far_b_ref, out_ref):
@@ -91,21 +91,37 @@
     )(owners, rank, own, near_a, near_b, far_a, far_b)
 
 
-def product_kernel(held_ref, left_ref, right_ref, update_ref):
+def product_kernel(held_ref, left_ref, right_ref, update_ref, made, sems):
     owner_count, slot_count, rows, order = held_ref.shape
+    strips = sems.shape[1]
+    height = order // strips
+    copies = []
     for s in range(slot_count):
         block = wide(held_ref[:, s]).reshape(order, order).astype(jnp.bfloat16)
         half = jnp.dot(left_ref[s], block, preferred_element_type=jnp.float32).astype(jnp.bfloat16)
-        full = jnp.dot(half, right_ref[s], preferred_element_type=jnp.float32)
-        update_ref[:, s] = full.reshape(owner_count, rows, order).astype(jnp.bfloat16)
+        for j in range(strips):
+            full = jnp.dot(
+                half[j * height : (j + 1) * height], right_ref[s], preferred_element_type=jnp.float32
+            )
+            run = pl.ds(j * height // rows, height // rows)
+            made[s, run] = full.reshape(height // rows, rows, order).astype(jnp.bfloat16)
+            copies.append(pltpu.make_async_copy(made.at[s, run], update_ref.at[run, s], sems.at[s, j]))
+            copies[-1].start()
+    for copy in copies:
+        copy.wait()
 
 
 def products(held, left_roots, right_roots):
+    owner_count, slot_count, rows, order = held.shape
     return pl.pallas_call(
         product_kernel,
         in_specs=[IN_VMEM] * 3,
-        out_specs=IN_VMEM,
+        out_specs=ANYWHERE,
         out_shape=jax.ShapeDtypeStruct(held.shape, jnp.bfloat16),
+        scratch_shapes=[
+            pltpu.VMEM((slot_count, owner_count, rows, order), jnp.bfloat16),
+            pltpu.SemaphoreType.DMA((slot_count, 2)),
+        ],
         compiler_params=pltpu.CompilerParams(vmem_limit_bytes=16 * MIB),
         cost_estimate=pl.CostEstimate(flops=2**30, bytes_accessed=4 * MIB, transcendentals=0),
     )(held, left_roots, right_roots)
@@ -183,15 +199,14 @@
     def start(bit, second):
         return (quarter ^ bit) * per_quarter + second * half
 
-    on_a, on_b, end_a, end_b = cut(
-        replica_rows, [start(2, 0), start(2, 1), start(1, 0), start(3, 1)], [half] * 4
-    )
+    on_a, on_b = cut(replica_rows, [start(2, 0), start(2, 1)], [half] * 2)
     on_a, on_b = swap(on_a, 1), swap(on_b, 3)
+    end_a, end_b = cut(replica_rows, [start(1, 0), start(3, 1)], [half] * 2)
     near_a, near_b = swap(end_a, 1), swap(end_b, 3)
     own, pass_a, pass_b = cut(
         replica_rows, [start(0, 0), start(3, 0), start(1, 1)], [per_quarter, half, half]
     )
-    on_a, on_b = add_pairs(pass_a, on_a, pass_b, on_b)
+    on_a, on_b = add(pass_a, on_a), add(pass_b, on_b)
     far_a, far_b = swap(on_a, 3), swap(on_b, 1)
 
     owners, rank = my_table(block_owners, quarter, per_quarter)

time: 107 us -> 105 us (0.981)
  local copies, waits for them, and re-layouts: 4.86 us -> 3.27 us
  Pallas kernels: 10.5 us -> 12 us
  waiting for transfers between devices: 34.2 us -> 32.8 us
    unnamed x14 -> x10, local copies, waits for them, and re-layouts: 4.79 us -> 3.19 us
    pallas_call x4 -> x6, Pallas kernels: 5.59 us -> 7.1 us  [the longest x3 4.93 us: cut(): pl.pallas_call(cut_kernel, in_specs=[IN_SMEM, IN_HBM], out_specs=[IN_VMEM...]
    ppermute x6, waiting for transfers between devices: 11.5 us -> 10.1 us  [swap(): return lax.ppermute(value, 'rep', [(i, i ^ bit) for i in range(rep_count)])]
  transfers between devices with their start and end apart: 7 -> 7, of which waited for: 5 -> 4; matrix products, arithmetic and copies ran while one was open for 0% -> 0% of each run, Pallas kernels for 4% -> 6%
where the time goes in v2:
time: 105 us
  blocking collectives  41.7 us (40%)
  waiting for transfers between devices  32.8 us (31%)
  starting transfers between devices  13.7 us (13%)
  Pallas kernels  12 us (11%)
  local copies, waits for them, and re-layouts  3.27 us (3%)
    all_to_all x1, blocking collectives, on_device(): lax.all_to_all(placed, 'fsdp', split_axis=0, concat_axis=0, tiled=True)  41.7 us
    all_to_all x1, waiting for transfers between devices, on_device(): lax.all_to_all(update_slots, 'fsdp', split_axis=0, concat_axis=0, tiled=T...  22.7 us
    ppermute x6, waiting for transfers between devices, swap(): return lax.ppermute(value, 'rep', [(i, i ^ bit) for i in range(rep_count)])  10.1 us
    ppermute x6, starting transfers between devices, swap(): return lax.ppermute(value, 'rep', [(i, i ^ bit) for i in range(rep_count)])  7.48 us
    all_to_all x1, starting transfers between devices, on_device(): lax.all_to_all(update_slots, 'fsdp', split_axis=0, concat_axis=0, tiled=T...  6.2 us
    pallas_call x3, Pallas kernels, cut(): pl.pallas_call(cut_kernel, in_specs=[IN_SMEM, IN_HBM], out_specs=[IN_VMEM...  4.93 us
    unnamed x10, local copies, waits for them, and re-layouts  3.19 us
    pallas_call x1, Pallas kernels, statistics(): pl.pallas_call(stats_kernel, grid=(slot_count,), in_specs=[pl.BlockSpec((...  2.65 us
  transfers between devices with their start and end apart: 7, of which 4 were waited for; matrix products, arithmetic and copies ran while one was open for 0% of the time, Pallas kernels for 6%

profile of v2, /device:TPU:1, one launch (start us, length us, event | category | flops | bytes accessed | tf_op | source)
XLA Modules:
  0.0 104.6 jit_solution(198064144641157344)
XLA Ops:
  0.6 0.0 copy-start
  0.7 0.1 pad_add_fusion.2.starts_ref
  0.7 1.6 %shard_map.87 = (bf16[32,8,512]{2,1,0:T(8,128)(2,1)S(1)}, bf16[32,8,512]{2,1,0:T(8,128)(2,1)S(1)}) custom-call(s32[2]{0:T(128)S(1)} %pad_add_fusion.2.starts_ref, bf16[256,8,512]{2,1,0:T(8,128)(2,1)} %bitcast.10), custom_call_target="tpu_custom_call" | custom-call | bytes 2097152 | tf_op jit(solution)/shard_map/pallas_call | solution.py:43
  2.3 2.2 %collective-permute-start.2 = (bf16[32,8,512]{2,1,0:T(8,128)(2,1)S(1)}, bf16[32,8,512]{2,1,0:T(8,128)(2,1)S(1)}, u32[]{:S(2)}, u32[]{:S(2)}) collective-permute-start(bf16[32,8,512]{2,1,0:T(8,128)(2,1)S(1)} %get-tuple-element.16), channel_id=1, source_target_pairs={{0,64},{64,0},{128,192},{192,128},{1,65},{65,1},{129,193},{193,129... | collective-permute-start | bytes 786440 | tf_op jit(solution)/shard_map/ppermute | solution.py:197
  4.5 1.9 %collective-permute-start.4 = (bf16[32,8,512]{2,1,0:T(8,128)(2,1)S(1)}, bf16[32,8,512]{2,1,0:T(8,128)(2,1)S(1)}, u32[]{:S(2)}, u32[]{:S(2)}) collective-permute-start(bf16[32,8,512]{2,1,0:T(8,128)(2,1)S(1)} %get-tuple-element.18), channel_id=1, source_target_pairs={{0,192},{64,128},{128,64},{192,0},{1,193},{65,129},{129,65},{193,1... | collective-permute-start | bytes 786440 | tf_op jit(solution)/shard_map/ppermute | solution.py:197
  6.4 0.1 pad_add_fusion.1.starts_ref
  6.5 1.6 %shard_map.86 = (bf16[32,8,512]{2,1,0:T(8,128)(2,1)S(1)}, bf16[32,8,512]{2,1,0:T(8,128)(2,1)S(1)}) custom-call(s32[2]{0:T(128)S(1)} %pad_add_fusion.1.starts_ref, bf16[256,8,512]{2,1,0:T(8,128)(2,1)} %bitcast.11), custom_call_target="tpu_custom_call" | custom-call | bytes 2097152 | tf_op jit(solution)/shard_map/pallas_call | solution.py:43
  8.1 0.5 collective-permute-start
  8.6 0.6 collective-permute-start.1
  9.2 0.1 pad_add_fusion.starts_ref
  9.3 1.8 %shard_map.85 = (bf16[64,8,512]{2,1,0:T(8,128)(2,1)S(1)}, bf16[32,8,512]{2,1,0:T(8,128)(2,1)S(1)}, bf16[32,8,512]{2,1,0:T(8,128)(2,1)S(1)}) custom-call(s32[3]{0:T(128)S(1)} %pad_add_fusion.starts_ref, bf16[256,8,512]{2,1,0:T(8,128)(2,1)} %bitcast.12), custom_call_target="tpu_custom_call" | custom-call | bytes 2097152 | tf_op jit(solution)/shard_map/pallas_call | solution.py:43
  11.0 0.0 collective-permute-done.2.b_ref
  11.1 0.1 shard_map.88
  11.1 2.2 %collective-permute-start.3 = (bf16[32,8,512]{2,1,0:T(8,128)(2,1)S(1)}, bf16[32,8,512]{2,1,0:T(8,128)(2,1)S(1)}, u32[]{:S(2)}, u32[]{:S(2)}) collective-permute-start(bf16[32,8,512]{2,1,0:T(8,128)(2,1)S(1)} %shard_map.88), channel_id=1, source_target_pairs={{0,192},{64,128},{128,64},{192,0},{1,193},{65,129},{129,65},{193,1... | collective-permute-start | bytes 786440 | tf_op jit(solution)/shard_map/ppermute | solution.py:197
  13.3 0.1 shard_map.89
  13.4 0.1 collective-permute-start.5
  13.5 0.1 dynamic-slice_bitcast_fusion.owner_ref
  13.6 0.2 convert_reduce_fusion.rank_ref
  13.8 2.5 %collective-permute-done.near_a_ref = bf16[32,8,512]{2,1,0:T(8,128)(2,1)S(1)} collective-permute-done((bf16[32,8,512]{2,1,0:T(8,128)(2,1)S(1)}, bf16[32,8,512]{2,1,0:T(8,128)(2,1)S(1)}, u32[]{:S(2)}, u32[]{:S(2)}) %collective-permute-start) | collective-permute-done | bytes 262176 | tf_op jit(solution)/shard_map/ppermute | solution.py:197
  16.2 2.0 %collective-permute-done.1.near_b_ref = bf16[32,8,512]{2,1,0:T(8,128)(2,1)S(1)} collective-permute-done((bf16[32,8,512]{2,1,0:T(8,128)(2,1)S(1)}, bf16[32,8,512]{2,1,0:T(8,128)(2,1)S(1)}, u32[]{:S(2)}, u32[]{:S(2)}) %collective-permute-start.1) | collective-permute-done | bytes 262176 | tf_op jit(solution)/shard_map/ppermute | solution.py:197
  18.2 5.6 %collective-permute-done.3.far_a_ref = bf16[32,8,512]{2,1,0:T(8,128)(2,1)S(1)} collective-permute-done((bf16[32,8,512]{2,1,0:T(8,128)(2,1)S(1)}, bf16[32,8,512]{2,1,0:T(8,128)(2,1)S(1)}, u32[]{:S(2)}, u32[]{:S(2)}) %collective-permute-start.3) | collective-permute-done | bytes 262176 | tf_op jit(solution)/shard_map/ppermute | solution.py:197
  23.8 0.0 collective-permute-done.5.far_b_ref
  23.8 0.8 shard_map.90
  24.7 41.7 %all_to_all.10.held_ref = bf16[64,2,8,512]{3,2,1,0:T(8,128)(2,1)S(1)} all-to-all(bf16[64,2,8,512]{3,2,1,0:T(8,128)(2,1)S(1)} %shard_map.90), channel_id=1, replica_groups=mesh['rep'=4,'fsdp'=64] {'fsdp'}, dimensions={0} | all-to-all | bytes 2097152 | tf_op jit(solution)/shard_map/all_to_all | solution.py:214
  66.4 2.0 %shard_map.91 = bf16[64,2,8,512]{3,2,1,0:T(8,128)(2,1)} custom-call(bf16[64,2,8,512]{3,2,1,0:T(8,128)(2,1)S(1)} %all_to_all.10.held_ref, bf16[2,512,512]{2,1,0:T(8,128)(2,1)S(1)} %copy-done.3, bf16[2,512,512]{2,1,0:T(8,128)(2,1)S(1)} %copy-done.4), custom_call_target="tpu_custom_call" | custom-call | flops 1073741824 | bytes 4194304 | tf_op jit(solution)/shard_map/pallas_call | solution.py:116
  68.4 6.2 %all-to-all-start.1 = ((bf16[64,2,8,512]{3,2,1,0:T(8,128)(2,1)}), bf16[64,2,8,512]{3,2,1,0:T(8,128)(2,1)S(1)}, u32[]{:S(2)}, u32[]{:S(2)}) async-start(bf16[64,2,8,512]{3,2,1,0:T(8,128)(2,1)} %shard_map.91), calls=%async_computation.1 | async-start | bytes 2097152 | tf_op jit(solution)/shard_map/all_to_all | solution.py:216
  74.6 0.0 copy-start.1
  74.7 1.6 %copy-done.1 = f32[2,512,512]{2,1,0:T(8,128)S(1)} copy-done((f32[2,512,512]{2,1,0:T(8,128)S(1)}, f32[2,512,512]{2,1,0:T(8,128)}, u32[]{:S(2)}) %copy-start.1) | copy-done | bytes 2097176
  76.2 1.6 %copy-done.2 = f32[2,512,512]{2,1,0:T(8,128)S(1)} copy-done((f32[2,512,512]{2,1,0:T(8,128)S(1)}, f32[2,512,512]{2,1,0:T(8,128)}, u32[]{:S(2)}) %copy-start.2) | copy-done | bytes 2097176
  77.8 2.6 %shard_map.93 = (f32[2,512,512]{2,1,0:T(8,128)}, f32[2,512,512]{2,1,0:T(8,128)}) custom-call(bf16[64,2,8,512]{3,2,1,0:T(8,128)(2,1)S(1)} %all_to_all.10.held_ref, f32[2,512,512]{2,1,0:T(8,128)S(1)} %copy-done.1, f32[2,512,512]{2,1,0:T(8,128)S(1)} %copy-done.2), custom_call_target="tpu_custom_call" | custom-call | flops 1073741824 | bytes 10485760 | tf_op jit(solution)/shard_map/pallas_call | solution.py:144
  80.5 22.7 %all-to-all-done.1.held_ref = bf16[64,2,8,512]{3,2,1,0:T(8,128)(2,1)S(1)} async-done(((bf16[64,2,8,512]{3,2,1,0:T(8,128)(2,1)}), bf16[64,2,8,512]{3,2,1,0:T(8,128)(2,1)S(1)}, u32[]{:S(2)}, u32[]{:S(2)}) %all-to-all-start.1) | async-done | bytes 1048608 | tf_op jit(solution)/shard_map/all_to_all | solution.py:216
  103.2 1.4 %shard_map.92 = bf16[64,8,512]{2,1,0:T(8,128)(2,1)} custom-call(s32[64]{0:T(128)S(1)} %dynamic-slice_bitcast_fusion.owner_ref, s32[64]{0:T(128)S(1)} %convert_reduce_fusion.rank_ref, bf16[64,2,8,512]{3,2,1,0:T(8,128)(2,1)S(1)} %all-to-all-done.1.held_ref), custom_call_target="tpu_custom_call" | custom-call | bytes 2097152 | tf_op jit(solution)/shard_map/pallas_call | solution.py:176
  (7 shorter events, 0.0 us)
Async XLA Ops:
  0.6 12.9 %copy-start = (s32[256,1]{0,1:T(1,128)S(1)}, s32[256,1]{0,1:T(1,128)}, u32[]{:S(2)}) copy-start(s32[256,1]{0,1:T(1,128)} %param.7) | copy-start | bytes 3076
  2.3 8.7 %collective-permute-start.2 = (bf16[32,8,512]{2,1,0:T(8,128)(2,1)S(1)}, bf16[32,8,512]{2,1,0:T(8,128)(2,1)S(1)}, u32[]{:S(2)}, u32[]{:S(2)}) collective-permute-start(bf16[32,8,512]{2,1,0:T(8,128)(2,1)S(1)} %get-tuple-element.16), channel_id=1, source_target_pairs={{0,64},{64,0},{128,192},{192,128},{1,65},{65,1},{129,193},{193,129... | collective-permute-start | bytes 786440 | tf_op jit(solution)/shard_map/ppermute | solution.py:197
  4.5 8.8 %collective-permute-start.4 = (bf16[32,8,512]{2,1,0:T(8,128)(2,1)S(1)}, bf16[32,8,512]{2,1,0:T(8,128)(2,1)S(1)}, u32[]{:S(2)}, u32[]{:S(2)}) collective-permute-start(bf16[32,8,512]{2,1,0:T(8,128)(2,1)S(1)} %get-tuple-element.18), channel_id=1, source_target_pairs={{0,192},{64,128},{128,64},{192,0},{1,193},{65,129},{129,65},{193,1... | collective-permute-start | bytes 786440 | tf_op jit(solution)/shard_map/ppermute | solution.py:197
  8.1 8.1 %collective-permute-start = (bf16[32,8,512]{2,1,0:T(8,128)(2,1)S(1)}, bf16[32,8,512]{2,1,0:T(8,128)(2,1)S(1)}, u32[]{:S(2)}, u32[]{:S(2)}) collective-permute-start(bf16[32,8,512]{2,1,0:T(8,128)(2,1)S(1)} %get-tuple-element.13), channel_id=1, source_target_pairs={{0,64},{64,0},{128,192},{192,128},{1,65},{65,1},{129,193},{193,129... | collective-permute-start | bytes 786440 | tf_op jit(solution)/shard_map/ppermute | solution.py:197
  8.6 9.6 %collective-permute-start.1 = (bf16[32,8,512]{2,1,0:T(8,128)(2,1)S(1)}, bf16[32,8,512]{2,1,0:T(8,128)(2,1)S(1)}, u32[]{:S(2)}, u32[]{:S(2)}) collective-permute-start(bf16[32,8,512]{2,1,0:T(8,128)(2,1)S(1)} %get-tuple-element.14), channel_id=1, source_target_pairs={{0,192},{64,128},{128,64},{192,0},{1,193},{65,129},{129,65},{193,1... | collective-permute-start | bytes 786440 | tf_op jit(solution)/shard_map/ppermute | solution.py:197
  11.1 12.7 %collective-permute-start.3 = (bf16[32,8,512]{2,1,0:T(8,128)(2,1)S(1)}, bf16[32,8,512]{2,1,0:T(8,128)(2,1)S(1)}, u32[]{:S(2)}, u32[]{:S(2)}) collective-permute-start(bf16[32,8,512]{2,1,0:T(8,128)(2,1)S(1)} %shard_map.88), channel_id=1, source_target_pairs={{0,192},{64,128},{128,64},{192,0},{1,193},{65,129},{129,65},{193,1... | collective-permute-start | bytes 786440 | tf_op jit(solution)/shard_map/ppermute | solution.py:197
  13.4 10.4 %collective-permute-start.5 = (bf16[32,8,512]{2,1,0:T(8,128)(2,1)S(1)}, bf16[32,8,512]{2,1,0:T(8,128)(2,1)S(1)}, u32[]{:S(2)}, u32[]{:S(2)}) collective-permute-start(bf16[32,8,512]{2,1,0:T(8,128)(2,1)S(1)} %shard_map.89), channel_id=1, source_target_pairs={{0,64},{64,0},{128,192},{192,128},{1,65},{65,1},{129,193},{193,129... | collective-permute-start | bytes 786440 | tf_op jit(solution)/shard_map/ppermute | solution.py:197
  23.8 42.6 %copy-start.3 = (bf16[2,512,512]{2,1,0:T(8,128)(2,1)S(1)}, bf16[2,512,512]{2,1,0:T(8,128)(2,1)}, u32[]{:S(2)}) copy-start(bf16[2,512,512]{2,1,0:T(8,128)(2,1)} %left_ref.2) | copy-start | bytes 3145732
  23.8 42.6 %copy-start.4 = (bf16[2,512,512]{2,1,0:T(8,128)(2,1)S(1)}, bf16[2,512,512]{2,1,0:T(8,128)(2,1)}, u32[]{:S(2)}) copy-start(bf16[2,512,512]{2,1,0:T(8,128)(2,1)} %right_ref.2) | copy-start | bytes 3145732
  68.4 34.8 %all-to-all-start.1 = ((bf16[64,2,8,512]{3,2,1,0:T(8,128)(2,1)}), bf16[64,2,8,512]{3,2,1,0:T(8,128)(2,1)S(1)}, u32[]{:S(2)}, u32[]{:S(2)}) async-start(bf16[64,2,8,512]{3,2,1,0:T(8,128)(2,1)} %shard_map.91), calls=%async_computation.1 | async-start | bytes 2097152 | tf_op jit(solution)/shard_map/all_to_all | solution.py:216
  74.6 1.6 %copy-start.1 = (f32[2,512,512]{2,1,0:T(8,128)S(1)}, f32[2,512,512]{2,1,0:T(8,128)}, u32[]{:S(2)}) copy-start(f32[2,512,512]{2,1,0:T(8,128)} %left_ref.3) | copy-start | bytes 6291460
  76.2 1.6 %copy-start.2 = (f32[2,512,512]{2,1,0:T(8,128)S(1)}, f32[2,512,512]{2,1,0:T(8,128)}, u32[]{:S(2)}) copy-start(f32[2,512,512]{2,1,0:T(8,128)} %right_ref.3) | copy-start | bytes 6291460

commit v3 on v2

--- a/solution.py
+++ b/solution.py
@@ -66,29 +66,46 @@
     )(a, b)
 
 
-def place_kernel(owner_ref, rank_ref, own_ref, near_a_ref, near_b_ref, far_a_ref, far_b_ref, out_ref):
+def near_kernel(own_ref, near_a_ref, near_b_ref, sum_ref):
+    half = near_a_ref.shape[0]
+    sum_ref[:half] = wide(own_ref[:half]) + wide(near_a_ref[...])
+    sum_ref[half:] = wide(own_ref[half:]) + wide(near_b_ref[...])
+
+
+def near_sum(own, near_a, near_b):
+    return pl.pallas_call(
+        near_kernel,
+        in_specs=[IN_VMEM] * 3,
+        out_specs=IN_VMEM,
+        out_shape=pltpu.VMEM(own.shape, jnp.float32),
+        compiler_params=pltpu.CompilerParams(vmem_limit_bytes=8 * MIB),
+        cost_estimate=pl.CostEstimate(flops=own.size, bytes_accessed=2 * MIB, transcendentals=0),
+    )(own, near_a, near_b)
+
+
+def place_kernel(owner_ref, rank_ref, near_ref, far_a_ref, far_b_ref, out_ref):
     out_ref[...] = jnp.zeros_like(out_ref)
-    half = near_a_ref.shape[0]
+    half = far_a_ref.shape[0]
 
     def step(i, carry):
-        for k, near, far in ((i, near_a_ref, far_a_ref), (i + half, near_b_ref, far_b_ref)):
-            total = wide(own_ref[k]) + wide(near[i]) + wide(far[i])
+        for k, far in ((i, far_a_ref), (i + half, far_b_ref)):
+            total = near_ref[k] + wide(far[i])
             out_ref[owner_ref[k], rank_ref[k]] = total.astype(jnp.bfloat16)
         return carry
 
-    lax.fori_loop(0, half, step, 0, unroll=4)
-
-
-def place(owners, rank, own, near_a, near_b, far_a, far_b, owner_count, slot_count):
-    shape = (owner_count, slot_count) + own.shape[1:]
+    lax.fori_loop(0, half, step, 0, unroll=8)
+
+
+def place(owners, rank, near, far_a, far_b, owner_count, slot_count):
+    shape = (owner_count, slot_count) + near.shape[1:]
     return pl.pallas_call(
         place_kernel,
-        in_specs=[IN_SMEM] * 2 + [IN_VMEM] * 5,
+        in_specs=[IN_SMEM] * 2 + [IN_VMEM] * 3,
         out_specs=IN_VMEM,
-        out_shape=jax.ShapeDtypeStruct(shape, jnp.bfloat16),
-        compiler_params=pltpu.CompilerParams(vmem_limit_bytes=8 * MIB),
-        cost_estimate=pl.CostEstimate(flops=2 * own.size, bytes_accessed=3 * MIB, transcendentals=0),
-    )(owners, rank, own, near_a, near_b, far_a, far_b)
+        out_shape=pltpu.VMEM(shape, jnp.bfloat16),
+        compiler_params=pltpu.CompilerParams(vmem_limit_bytes=8 * MIB),
+        cost_estimate=pl.CostEstimate(flops=near.size, bytes_accessed=3 * MIB, transcendentals=0),
+    )(owners, rank, near, far_a, far_b)
 
 
 def product_kernel(held_ref, left_ref, right_ref, update_ref, made, sems):
@@ -199,7 +216,8 @@
     def start(bit, second):
         return (quarter ^ bit) * per_quarter + second * half
 
-    on_a, on_b = cut(replica_rows, [start(2, 0), start(2, 1)], [half] * 2)
+    on_a = lax.dynamic_slice_in_dim(replica_rows, start(2, 0), half)
+    on_b = lax.dynamic_slice_in_dim(replica_rows, start(2, 1), half)
     on_a, on_b = swap(on_a, 1), swap(on_b, 3)
     end_a, end_b = cut(replica_rows, [start(1, 0), start(3, 1)], [half] * 2)
     near_a, near_b = swap(end_a, 1), swap(end_b, 3)
@@ -210,7 +228,8 @@
     far_a, far_b = swap(on_a, 3), swap(on_b, 1)
 
     owners, rank = my_table(block_owners, quarter, per_quarter)
-    placed = place(owners, rank, own, near_a, near_b, far_a, far_b, owner_count, slot_count)
+    near = near_sum(own, near_a, near_b)
+    placed = place(owners, rank, near, far_a, far_b, owner_count, slot_count)
     held = lax.all_to_all(placed, "fsdp", split_axis=0, concat_axis=0, tiled=True)
     update_slots = products(held, left_roots, right_roots)
     returned = lax.all_to_all(update_slots, "fsdp", split_axis=0, concat_axis=0, tiled=True)

time: 105 us -> 104 us (level)
  Pallas kernels: 12 us -> 10.4 us
  local copies, waits for them, and re-layouts: 3.27 us -> 4.35 us
    pallas_call x3 -> x2, Pallas kernels: 4.93 us -> 3.34 us  [cut(): pl.pallas_call(cut_kernel, in_specs=[IN_SMEM, IN_HBM], out_specs=[IN_VMEM...]
    dynamic_slice x0 -> x1, local copies, waits for them, and re-layouts: none -> 1.07 us  [on_device(): on_b = lax.dynamic_slice_in_dim(replica_rows, start(2, 1), half)]
where the time goes in v3:
time: 104 us
  blocking collectives  41.7 us (40%)
  waiting for transfers between devices  32.7 us (31%)
  starting transfers between devices  13.7 us (13%)
  Pallas kernels  10.4 us (10%)
  local copies, waits for them, and re-layouts  4.35 us (4%)
    all_to_all x1, blocking collectives, on_device(): lax.all_to_all(placed, 'fsdp', split_axis=0, concat_axis=0, tiled=True)  41.7 us
    all_to_all x1, waiting for transfers between devices, on_device(): lax.all_to_all(update_slots, 'fsdp', split_axis=0, concat_axis=0, tiled=T...  22.7 us
    ppermute x6, waiting for transfers between devices, swap(): return lax.ppermute(value, 'rep', [(i, i ^ bit) for i in range(rep_count)])  9.93 us
    ppermute x6, starting transfers between devices, swap(): return lax.ppermute(value, 'rep', [(i, i ^ bit) for i in range(rep_count)])  7.48 us
    all_to_all x1, starting transfers between devices, on_device(): lax.all_to_all(update_slots, 'fsdp', split_axis=0, concat_axis=0, tiled=T...  6.21 us
    pallas_call x2, Pallas kernels, cut(): pl.pallas_call(cut_kernel, in_specs=[IN_SMEM, IN_HBM], out_specs=[IN_VMEM...  3.34 us
    unnamed x10, local copies, waits for them, and re-layouts  3.2 us
    pallas_call x1, Pallas kernels, statistics(): pl.pallas_call(stats_kernel, grid=(slot_count,), in_specs=[pl.BlockSpec((...  2.63 us
  transfers between devices with their start and end apart: 7, of which 4 were waited for; matrix products, arithmetic and copies ran while one was open for 0% of the time, Pallas kernels for 6%

profile of v3, /device:TPU:1, one launch (start us, length us, event | category | flops | bytes accessed | tf_op | source)
XLA Modules:
  0.0 104.0 jit_solution(2428454597987314834)
XLA Ops:
  0.6 0.0 copy-start
  0.7 1.1 %dynamic-slice_bitcast_fusion = (bf16[32,8,512]{2,1,0:T(8,128)(2,1)S(1)}, bf16[32,8,512]{2,1,0:T(8,128)(2,1)S(1)}) fusion(bf16[1,256,8,512]{3,2,1,0:T(8,128)(2,1)} %param.6, s32[]{:T(128)S(6)} %select_n.11, s32[]{:T(128)S(6)} %select_n.10), kind=kLoop, calls=%fused_computation | loop fusion | bytes 1048584 | tf_op jit(solution)/shard_map/dynamic_slice | solution.py:220
  1.7 2.2 %collective-permute-start.2 = (bf16[32,8,512]{2,1,0:T(8,128)(2,1)S(1)}, bf16[32,8,512]{2,1,0:T(8,128)(2,1)S(1)}, u32[]{:S(2)}, u32[]{:S(2)}) collective-permute-start(bf16[32,8,512]{2,1,0:T(8,128)(2,1)S(1)} %get-tuple-element.18), channel_id=1, source_target_pairs={{0,64},{64,0},{128,192},{192,128},{1,65},{65,1},{129,193},{193,129... | collective-permute-start | bytes 786440 | tf_op jit(solution)/shard_map/ppermute | solution.py:214
  3.9 1.9 %collective-permute-start.4 = (bf16[32,8,512]{2,1,0:T(8,128)(2,1)S(1)}, bf16[32,8,512]{2,1,0:T(8,128)(2,1)S(1)}, u32[]{:S(2)}, u32[]{:S(2)}) collective-permute-start(bf16[32,8,512]{2,1,0:T(8,128)(2,1)S(1)} %get-tuple-element.17), channel_id=1, source_target_pairs={{0,192},{64,128},{128,64},{192,0},{1,193},{65,129},{129,65},{193,1... | collective-permute-start | bytes 786440 | tf_op jit(solution)/shard_map/ppermute | solution.py:214
  5.8 0.1 pad_add_fusion.1.starts_ref
  5.9 1.6 %shard_map.86 = (bf16[32,8,512]{2,1,0:T(8,128)(2,1)S(1)}, bf16[32,8,512]{2,1,0:T(8,128)(2,1)S(1)}) custom-call(s32[2]{0:T(128)S(1)} %pad_add_fusion.1.starts_ref, bf16[256,8,512]{2,1,0:T(8,128)(2,1)} %bitcast.12), custom_call_target="tpu_custom_call" | custom-call | bytes 2097152 | tf_op jit(solution)/shard_map/pallas_call | solution.py:43
  7.5 0.5 collective-permute-start
  8.0 0.6 collective-permute-start.1
  8.6 0.1 pad_add_fusion.starts_ref
  8.7 1.8 %shard_map.85 = (bf16[64,8,512]{2,1,0:T(8,128)(2,1)S(1)}, bf16[32,8,512]{2,1,0:T(8,128)(2,1)S(1)}, bf16[32,8,512]{2,1,0:T(8,128)(2,1)S(1)}) custom-call(s32[3]{0:T(128)S(1)} %pad_add_fusion.starts_ref, bf16[256,8,512]{2,1,0:T(8,128)(2,1)} %bitcast.13), custom_call_target="tpu_custom_call" | custom-call | bytes 2097152 | tf_op jit(solution)/shard_map/pallas_call | solution.py:43
  10.5 0.1 shard_map.88
  10.5 2.2 %collective-permute-start.3 = (bf16[32,8,512]{2,1,0:T(8,128)(2,1)S(1)}, bf16[32,8,512]{2,1,0:T(8,128)(2,1)S(1)}, u32[]{:S(2)}, u32[]{:S(2)}) collective-permute-start(bf16[32,8,512]{2,1,0:T(8,128)(2,1)S(1)} %shard_map.88), channel_id=1, source_target_pairs={{0,192},{64,128},{128,64},{192,0},{1,193},{65,129},{129,65},{193,1... | collective-permute-start | bytes 786440 | tf_op jit(solution)/shard_map/ppermute | solution.py:214
  12.7 0.1 shard_map.89
  12.8 0.1 collective-permute-start.5
  12.9 0.1 fusion.1.owner_ref
  13.0 0.2 convert_reduce_fusion.rank_ref
  13.2 2.5 %collective-permute-done.near_a_ref = bf16[32,8,512]{2,1,0:T(8,128)(2,1)S(1)} collective-permute-done((bf16[32,8,512]{2,1,0:T(8,128)(2,1)S(1)}, bf16[32,8,512]{2,1,0:T(8,128)(2,1)S(1)}, u32[]{:S(2)}, u32[]{:S(2)}) %collective-permute-start) | collective-permute-done | bytes 262176 | tf_op jit(solution)/shard_map/ppermute | solution.py:214
  15.6 2.0 %collective-permute-done.1.near_b_ref = bf16[32,8,512]{2,1,0:T(8,128)(2,1)S(1)} collective-permute-done((bf16[32,8,512]{2,1,0:T(8,128)(2,1)S(1)}, bf16[32,8,512]{2,1,0:T(8,128)(2,1)S(1)}, u32[]{:S(2)}, u32[]{:S(2)}) %collective-permute-start.1) | collective-permute-done | bytes 262176 | tf_op jit(solution)/shard_map/ppermute | solution.py:214
  17.6 0.1 shard_map.87.near_ref
  17.7 0.0 copy-start.3
  17.7 0.0 copy-start.4
  17.7 5.5 %collective-permute-done.3.far_a_ref = bf16[32,8,512]{2,1,0:T(8,128)(2,1)S(1)} collective-permute-done((bf16[32,8,512]{2,1,0:T(8,128)(2,1)S(1)}, bf16[32,8,512]{2,1,0:T(8,128)(2,1)S(1)}, u32[]{:S(2)}, u32[]{:S(2)}) %collective-permute-start.3) | collective-permute-done | bytes 262176 | tf_op jit(solution)/shard_map/ppermute | solution.py:214
  23.2 0.8 shard_map.90
  24.0 41.7 %all_to_all.10.held_ref = bf16[64,2,8,512]{3,2,1,0:T(8,128)(2,1)S(1)} all-to-all(bf16[64,2,8,512]{3,2,1,0:T(8,128)(2,1)S(1)} %shard_map.90), channel_id=1, replica_groups=mesh['rep'=4,'fsdp'=64] {'fsdp'}, dimensions={0} | all-to-all | bytes 2097152 | tf_op jit(solution)/shard_map/all_to_all | solution.py:233
  65.7 2.0 %shard_map.91 = bf16[64,2,8,512]{3,2,1,0:T(8,128)(2,1)} custom-call(bf16[64,2,8,512]{3,2,1,0:T(8,128)(2,1)S(1)} %all_to_all.10.held_ref, bf16[2,512,512]{2,1,0:T(8,128)(2,1)S(1)} %copy-done.3, bf16[2,512,512]{2,1,0:T(8,128)(2,1)S(1)} %copy-done.4), custom_call_target="tpu_custom_call" | custom-call | flops 1073741824 | bytes 4194304 | tf_op jit(solution)/shard_map/pallas_call | solution.py:133
  67.8 6.2 %all-to-all-start.1 = ((bf16[64,2,8,512]{3,2,1,0:T(8,128)(2,1)}), bf16[64,2,8,512]{3,2,1,0:T(8,128)(2,1)S(1)}, u32[]{:S(2)}, u32[]{:S(2)}) async-start(bf16[64,2,8,512]{3,2,1,0:T(8,128)(2,1)} %shard_map.91), calls=%async_computation.1 | async-start | bytes 2097152 | tf_op jit(solution)/shard_map/all_to_all | solution.py:235
  74.0 0.0 copy-start.1
  74.0 1.6 %copy-done.1 = f32[2,512,512]{2,1,0:T(8,128)S(1)} copy-done((f32[2,512,512]{2,1,0:T(8,128)S(1)}, f32[2,512,512]{2,1,0:T(8,128)}, u32[]{:S(2)}) %copy-start.1) | copy-done | bytes 2097176
  75.6 1.6 %copy-done.2 = f32[2,512,512]{2,1,0:T(8,128)S(1)} copy-done((f32[2,512,512]{2,1,0:T(8,128)S(1)}, f32[2,512,512]{2,1,0:T(8,128)}, u32[]{:S(2)}) %copy-start.2) | copy-done | bytes 2097176
  77.2 2.6 %shard_map.93 = (f32[2,512,512]{2,1,0:T(8,128)}, f32[2,512,512]{2,1,0:T(8,128)}) custom-call(bf16[64,2,8,512]{3,2,1,0:T(8,128)(2,1)S(1)} %all_to_all.10.held_ref, f32[2,512,512]{2,1,0:T(8,128)S(1)} %copy-done.1, f32[2,512,512]{2,1,0:T(8,128)S(1)} %copy-done.2), custom_call_target="tpu_custom_call" | custom-call | flops 1073741824 | bytes 10485760 | tf_op jit(solution)/shard_map/pallas_call | solution.py:161
  79.8 22.7 %all-to-all-done.1.held_ref = bf16[64,2,8,512]{3,2,1,0:T(8,128)(2,1)S(1)} async-done(((bf16[64,2,8,512]{3,2,1,0:T(8,128)(2,1)}), bf16[64,2,8,512]{3,2,1,0:T(8,128)(2,1)S(1)}, u32[]{:S(2)}, u32[]{:S(2)}) %all-to-all-start.1) | async-done | bytes 1048608 | tf_op jit(solution)/shard_map/all_to_all | solution.py:235
  102.5 1.4 %shard_map.92 = bf16[64,8,512]{2,1,0:T(8,128)(2,1)} custom-call(s32[64]{0:T(128)S(1)} %fusion.1.owner_ref, s32[64]{0:T(128)S(1)} %convert_reduce_fusion.rank_ref, bf16[64,2,8,512]{3,2,1,0:T(8,128)(2,1)S(1)} %all-to-all-done.1.held_ref), custom_call_target="tpu_custom_call" | custom-call | bytes 2097152 | tf_op jit(solution)/shard_map/pallas_call | solution.py:193
  (7 shorter events, 0.0 us)
Async XLA Ops:
  0.6 12.3 %copy-start = (s32[256,1]{0,1:T(1,128)S(1)}, s32[256,1]{0,1:T(1,128)}, u32[]{:S(2)}) copy-start(s32[256,1]{0,1:T(1,128)} %param.7) | copy-start | bytes 3076
  1.7 8.7 %collective-permute-start.2 = (bf16[32,8,512]{2,1,0:T(8,128)(2,1)S(1)}, bf16[32,8,512]{2,1,0:T(8,128)(2,1)S(1)}, u32[]{:S(2)}, u32[]{:S(2)}) collective-permute-start(bf16[32,8,512]{2,1,0:T(8,128)(2,1)S(1)} %get-tuple-element.18), channel_id=1, source_target_pairs={{0,64},{64,0},{128,192},{192,128},{1,65},{65,1},{129,193},{193,129... | collective-permute-start | bytes 786440 | tf_op jit(solution)/shard_map/ppermute | solution.py:214
  3.9 8.8 %collective-permute-start.4 = (bf16[32,8,512]{2,1,0:T(8,128)(2,1)S(1)}, bf16[32,8,512]{2,1,0:T(8,128)(2,1)S(1)}, u32[]{:S(2)}, u32[]{:S(2)}) collective-permute-start(bf16[32,8,512]{2,1,0:T(8,128)(2,1)S(1)} %get-tuple-element.17), channel_id=1, source_target_pairs={{0,192},{64,128},{128,64},{192,0},{1,193},{65,129},{129,65},{193,1... | collective-permute-start | bytes 786440 | tf_op jit(solution)/shard_map/ppermute | solution.py:214
  7.5 8.1 %collective-permute-start = (bf16[32,8,512]{2,1,0:T(8,128)(2,1)S(1)}, bf16[32,8,512]{2,1,0:T(8,128)(2,1)S(1)}, u32[]{:S(2)}, u32[]{:S(2)}) collective-permute-start(bf16[32,8,512]{2,1,0:T(8,128)(2,1)S(1)} %get-tuple-element.11), channel_id=1, source_target_pairs={{0,64},{64,0},{128,192},{192,128},{1,65},{65,1},{129,193},{193,129... | collective-permute-start | bytes 786440 | tf_op jit(solution)/shard_map/ppermute | solution.py:214
  8.0 9.6 %collective-permute-start.1 = (bf16[32,8,512]{2,1,0:T(8,128)(2,1)S(1)}, bf16[32,8,512]{2,1,0:T(8,128)(2,1)S(1)}, u32[]{:S(2)}, u32[]{:S(2)}) collective-permute-start(bf16[32,8,512]{2,1,0:T(8,128)(2,1)S(1)} %get-tuple-element.12), channel_id=1, source_target_pairs={{0,192},{64,128},{128,64},{192,0},{1,193},{65,129},{129,65},{193,1... | collective-permute-start | bytes 786440 | tf_op jit(solution)/shard_map/ppermute | solution.py:214
  10.5 12.7 %collective-permute-start.3 = (bf16[32,8,512]{2,1,0:T(8,128)(2,1)S(1)}, bf16[32,8,512]{2,1,0:T(8,128)(2,1)S(1)}, u32[]{:S(2)}, u32[]{:S(2)}) collective-permute-start(bf16[32,8,512]{2,1,0:T(8,128)(2,1)S(1)} %shard_map.88), channel_id=1, source_target_pairs={{0,192},{64,128},{128,64},{192,0},{1,193},{65,129},{129,65},{193,1... | collective-permute-start | bytes 786440 | tf_op jit(solution)/shard_map/ppermute | solution.py:214
  12.8 10.4 %collective-permute-start.5 = (bf16[32,8,512]{2,1,0:T(8,128)(2,1)S(1)}, bf16[32,8,512]{2,1,0:T(8,128)(2,1)S(1)}, u32[]{:S(2)}, u32[]{:S(2)}) collective-permute-start(bf16[32,8,512]{2,1,0:T(8,128)(2,1)S(1)} %shard_map.89), channel_id=1, source_target_pairs={{0,64},{64,0},{128,192},{192,128},{1,65},{65,1},{129,193},{193,129... | collective-permute-start | bytes 786440 | tf_op jit(solution)/shard_map/ppermute | solution.py:214
  17.7 48.0 %copy-start.3 = (bf16[2,512,512]{2,1,0:T(8,128)(2,1)S(1)}, bf16[2,512,512]{2,1,0:T(8,128)(2,1)}, u32[]{:S(2)}) copy-start(bf16[2,512,512]{2,1,0:T(8,128)(2,1)} %left_ref.2) | copy-start | bytes 3145732
  17.7 48.0 %copy-start.4 = (bf16[2,512,512]{2,1,0:T(8,128)(2,1)S(1)}, bf16[2,512,512]{2,1,0:T(8,128)(2,1)}, u32[]{:S(2)}) copy-start(bf16[2,512,512]{2,1,0:T(8,128)(2,1)} %right_ref.2) | copy-start | bytes 3145732
  67.8 34.8 %all-to-all-start.1 = ((bf16[64,2,8,512]{3,2,1,0:T(8,128)(2,1)}), bf16[64,2,8,512]{3,2,1,0:T(8,128)(2,1)S(1)}, u32[]{:S(2)}, u32[]{:S(2)}) async-start(bf16[64,2,8,512]{3,2,1,0:T(8,128)(2,1)} %shard_map.91), calls=%async_computation.1 | async-start | bytes 2097152 | tf_op jit(solution)/shard_map/all_to_all | solution.py:235
  74.0 1.6 %copy-start.1 = (f32[2,512,512]{2,1,0:T(8,128)S(1)}, f32[2,512,512]{2,1,0:T(8,128)}, u32[]{:S(2)}) copy-start(f32[2,512,512]{2,1,0:T(8,128)} %left_ref.3) | copy-start | bytes 6291460
  75.6 1.6 %copy-start.2 = (f32[2,512,512]{2,1,0:T(8,128)S(1)}, f32[2,512,512]{2,1,0:T(8,128)}, u32[]{:S(2)}) copy-start(f32[2,512,512]{2,1,0:T(8,128)} %right_ref.3) | copy-start | bytes 6291460

commit v4 on v3

--- a/solution.py
+++ b/solution.py
@@ -12,14 +12,14 @@
 IN_HBM = pl.BlockSpec(memory_space=pltpu.HBM)
 
 
-def my_table(block_owners, quarter, per_quarter):
+def my_places(block_owners, quarter, per_quarter, slot_count):
     owners = lax.dynamic_slice(block_owners, (quarter * per_quarter, 0), (per_quarter, 1))
     same_owner = owners == owners.reshape(1, per_quarter)
     earlier = lax.broadcasted_iota(jnp.int32, (per_quarter, per_quarter), 1) < lax.broadcasted_iota(
         jnp.int32, (per_quarter, per_quarter), 0
     )
     rank = jnp.sum((same_owner & earlier).astype(jnp.int32), axis=1)
-    return owners[:, 0], rank
+    return owners[:, 0] * slot_count + rank
 
 
 def wide(value):
@@ -83,29 +83,29 @@
     )(own, near_a, near_b)
 
 
-def place_kernel(owner_ref, rank_ref, near_ref, far_a_ref, far_b_ref, out_ref):
+def place_kernel(place_ref, near_ref, far_a_ref, far_b_ref, out_ref):
     out_ref[...] = jnp.zeros_like(out_ref)
     half = far_a_ref.shape[0]
 
     def step(i, carry):
         for k, far in ((i, far_a_ref), (i + half, far_b_ref)):
             total = near_ref[k] + wide(far[i])
-            out_ref[owner_ref[k], rank_ref[k]] = total.astype(jnp.bfloat16)
+            out_ref[place_ref[k]] = total.astype(jnp.bfloat16)
         return carry
 
     lax.fori_loop(0, half, step, 0, unroll=8)
 
 
-def place(owners, rank, near, far_a, far_b, owner_count, slot_count):
-    shape = (owner_count, slot_count) + near.shape[1:]
+def place(places, near, far_a, far_b, place_count):
+    shape = (place_count,) + near.shape[1:]
     return pl.pallas_call(
         place_kernel,
-        in_specs=[IN_SMEM] * 2 + [IN_VMEM] * 3,
+        in_specs=[IN_SMEM] + [IN_VMEM] * 3,
         out_specs=IN_VMEM,
-        out_shape=pltpu.VMEM(shape, jnp.bfloat16),
+        out_shape=jax.ShapeDtypeStruct(shape, jnp.bfloat16),
         compiler_params=pltpu.CompilerParams(vmem_limit_bytes=8 * MIB),
         cost_estimate=pl.CostEstimate(flops=near.size, bytes_accessed=3 * MIB, transcendentals=0),
-    )(owners, rank, near, far_a, far_b)
+    )(places, near, far_a, far_b)
 
 
 def product_kernel(held_ref, left_ref, right_ref, update_ref, made, sems):
@@ -169,7 +169,7 @@
     )(held, left_stats, right_stats)
 
 
-def take_kernel(owner_ref, rank_ref, held_ref, out_ref, gathered, sems):
+def take_kernel(place_ref, held_ref, out_ref, gathered, sems):
     count = gathered.shape[0]
     parts = sems.shape[0]
     size = count // parts
@@ -177,10 +177,10 @@
     for part in range(parts):
         def step(i, carry):
             k = part * size + i
-            gathered[k] = held_ref[owner_ref[k], rank_ref[k]]
+            gathered[k] = held_ref[place_ref[k]]
             return carry
 
-        lax.fori_loop(0, size, step, 0, unroll=8)
+        lax.fori_loop(0, size, step, 0, unroll=32)
         run = pl.ds(part * size, size)
         copies.append(pltpu.make_async_copy(gathered.at[run], out_ref.at[run], sems.at[part]))
         copies[-1].start()
@@ -188,17 +188,17 @@
         copy.wait()
 
 
-def take(owners, rank, held):
-    shape = (owners.shape[0],) + held.shape[2:]
+def take(places, held):
+    shape = places.shape + held.shape[1:]
     return pl.pallas_call(
         take_kernel,
-        in_specs=[IN_SMEM] * 2 + [IN_VMEM],
+        in_specs=[IN_SMEM, IN_VMEM],
         out_specs=ANYWHERE,
         out_shape=jax.ShapeDtypeStruct(shape, jnp.bfloat16),
-        scratch_shapes=[pltpu.VMEM(shape, jnp.bfloat16), pltpu.SemaphoreType.DMA((4,))],
+        scratch_shapes=[pltpu.VMEM(shape, jnp.bfloat16), pltpu.SemaphoreType.DMA((2,))],
         compiler_params=pltpu.CompilerParams(vmem_limit_bytes=8 * MIB),
         cost_estimate=pl.CostEstimate(flops=0, bytes_accessed=2 * MIB, transcendentals=0),
-    )(owners, rank, held)
+    )(places, held)
 
 
 def on_device(gradients, block_owners, left_stats, right_stats, left_roots, right_roots):
@@ -227,14 +227,15 @@
     on_a, on_b = add(pass_a, on_a), add(pass_b, on_b)
     far_a, far_b = swap(on_a, 3), swap(on_b, 1)
 
-    owners, rank = my_table(block_owners, quarter, per_quarter)
+    places = my_places(block_owners, quarter, per_quarter, slot_count)
     near = near_sum(own, near_a, near_b)
-    placed = place(owners, rank, near, far_a, far_b, owner_count, slot_count)
+    placed = place(places, near, far_a, far_b, owner_count * slot_count)
+    placed = placed.reshape((owner_count, slot_count) + placed.shape[1:])
     held = lax.all_to_all(placed, "fsdp", split_axis=0, concat_axis=0, tiled=True)
     update_slots = products(held, left_roots, right_roots)
     returned = lax.all_to_all(update_slots, "fsdp", split_axis=0, concat_axis=0, tiled=True)
     left_new, right_new = statistics(held, left_stats, right_stats)
-    update = take(owners, rank, returned)
+    update = take(places, returned.reshape((-1,) + returned.shape[2:]))
     return (update, left_new, right_new)
 
 

time: 104 us -> 104 us (level)
  waiting for transfers between devices: 32.7 us -> 33.9 us
    ppermute x6, waiting for transfers between devices: 9.93 us -> 11.1 us  [swap(): return lax.ppermute(value, 'rep', [(i, i ^ bit) for i in range(rep_count)])]
  transfers between devices with their start and end apart: 7 -> 7, of which waited for: 4 -> 5; matrix products, arithmetic and copies ran while one was open for 0% -> 0% of each run, Pallas kernels for 6% -> 6%
where the time goes in v4:
time: 104 us
  blocking collectives  41.7 us (40%)
  waiting for transfers between devices  33.9 us (33%)
  starting transfers between devices  12.7 us (12%)
  Pallas kernels  10.3 us (10%)
  local copies, waits for them, and re-layouts  4.34 us (4%)
    all_to_all x1, blocking collectives, on_device(): lax.all_to_all(placed, 'fsdp', split_axis=0, concat_axis=0, tiled=True)  41.7 us
    all_to_all x1, waiting for transfers between devices, on_device(): lax.all_to_all(update_slots, 'fsdp', split_axis=0, concat_axis=0, tiled=T...  22.7 us
    ppermute x6, waiting for transfers between devices, swap(): return lax.ppermute(value, 'rep', [(i, i ^ bit) for i in range(rep_count)])  11.1 us
    ppermute x6, starting transfers between devices, swap(): return lax.ppermute(value, 'rep', [(i, i ^ bit) for i in range(rep_count)])  6.46 us
    all_to_all x1, starting transfers between devices, on_device(): lax.all_to_all(update_slots, 'fsdp', split_axis=0, concat_axis=0, tiled=T...  6.21 us
    pallas_call x2, Pallas kernels, cut(): pl.pallas_call(cut_kernel, in_specs=[IN_SMEM, IN_HBM], out_specs=[IN_VMEM...  3.35 us
    unnamed x10, local copies, waits for them, and re-layouts  3.19 us
    pallas_call x1, Pallas kernels, statistics(): pl.pallas_call(stats_kernel, grid=(slot_count,), in_specs=[pl.BlockSpec((...  2.65 us
  transfers between devices with their start and end apart: 7, of which 5 were waited for; matrix products, arithmetic and copies ran while one was open for 0% of the time, Pallas kernels for 6%

profile of v4, /device:TPU:1, one launch (start us, length us, event | category | flops | bytes accessed | tf_op | source)
XLA Modules:
  0.0 104.1 jit_solution(5796462397340570112)
XLA Ops:
  0.6 1.1 %dynamic-slice_bitcast_fusion = (bf16[32,8,512]{2,1,0:T(8,128)(2,1)S(1)}, bf16[32,8,512]{2,1,0:T(8,128)(2,1)S(1)}) fusion(bf16[1,256,8,512]{3,2,1,0:T(8,128)(2,1)} %param.6, s32[]{:T(128)S(6)} %select_n.11, s32[]{:T(128)S(6)} %select_n.10), kind=kLoop, calls=%fused_computation | loop fusion | bytes 1048584 | tf_op jit(solution)/shard_map/dynamic_slice | solution.py:220
  1.7 3.7 %collective-permute-start.4 = (bf16[32,8,512]{2,1,0:T(8,128)(2,1)S(1)}, bf16[32,8,512]{2,1,0:T(8,128)(2,1)S(1)}, u32[]{:S(2)}, u32[]{:S(2)}) collective-permute-start(bf16[32,8,512]{2,1,0:T(8,128)(2,1)S(1)} %get-tuple-element.17), channel_id=1, source_target_pairs={{0,192},{64,128},{128,64},{192,0},{1,193},{65,129},{129,65},{193,1... | collective-permute-start | bytes 786440 | tf_op jit(solution)/shard_map/ppermute | solution.py:214
  5.4 0.1 pad_add_fusion.1.starts_ref
  5.4 1.6 %shard_map.86 = (bf16[32,8,512]{2,1,0:T(8,128)(2,1)S(1)}, bf16[32,8,512]{2,1,0:T(8,128)(2,1)S(1)}) custom-call(s32[2]{0:T(128)S(1)} %pad_add_fusion.1.starts_ref, bf16[256,8,512]{2,1,0:T(8,128)(2,1)} %bitcast.18), custom_call_target="tpu_custom_call" | custom-call | bytes 2097152 | tf_op jit(solution)/shard_map/pallas_call | solution.py:43
  7.0 1.5 %collective-permute-start = (bf16[32,8,512]{2,1,0:T(8,128)(2,1)S(1)}, bf16[32,8,512]{2,1,0:T(8,128)(2,1)S(1)}, u32[]{:S(2)}, u32[]{:S(2)}) collective-permute-start(bf16[32,8,512]{2,1,0:T(8,128)(2,1)S(1)} %get-tuple-element.11), channel_id=1, source_target_pairs={{0,64},{64,0},{128,192},{192,128},{1,65},{65,1},{129,193},{193,129... | collective-permute-start | bytes 786440 | tf_op jit(solution)/shard_map/ppermute | solution.py:214
  8.6 0.1 collective-permute-start.1
  8.7 0.1 pad_add_fusion.starts_ref
  8.8 1.8 %shard_map.85 = (bf16[64,8,512]{2,1,0:T(8,128)(2,1)S(1)}, bf16[32,8,512]{2,1,0:T(8,128)(2,1)S(1)}, bf16[32,8,512]{2,1,0:T(8,128)(2,1)S(1)}) custom-call(s32[3]{0:T(128)S(1)} %pad_add_fusion.starts_ref, bf16[256,8,512]{2,1,0:T(8,128)(2,1)} %bitcast.19), custom_call_target="tpu_custom_call" | custom-call | bytes 2097152 | tf_op jit(solution)/shard_map/pallas_call | solution.py:43
  10.5 0.1 fusion.1
  10.6 1.6 %collective-permute-done.2.b_ref = bf16[32,8,512]{2,1,0:T(8,128)(2,1)S(1)} collective-permute-done((bf16[32,8,512]{2,1,0:T(8,128)(2,1)S(1)}, bf16[32,8,512]{2,1,0:T(8,128)(2,1)S(1)}, u32[]{:S(2)}, u32[]{:S(2)}) %collective-permute-start.2) | collective-permute-done | bytes 262176 | tf_op jit(solution)/shard_map/ppermute | solution.py:214
  12.2 0.1 shard_map.88
  12.3 1.1 %collective-permute-start.3 = (bf16[32,8,512]{2,1,0:T(8,128)(2,1)S(1)}, bf16[32,8,512]{2,1,0:T(8,128)(2,1)S(1)}, u32[]{:S(2)}, u32[]{:S(2)}) collective-permute-start(bf16[32,8,512]{2,1,0:T(8,128)(2,1)S(1)} %shard_map.88), channel_id=1, source_target_pairs={{0,192},{64,128},{128,64},{192,0},{1,193},{65,129},{129,65},{193,1... | collective-permute-start | bytes 786440 | tf_op jit(solution)/shard_map/ppermute | solution.py:214
  13.4 0.1 shard_map.89
  13.4 0.1 collective-permute-start.5
  13.5 0.2 convert_reduce_fusion
  13.7 0.1 multiply_add_fusion.place_ref
  13.8 4.1 %collective-permute-done.near_a_ref = bf16[32,8,512]{2,1,0:T(8,128)(2,1)S(1)} collective-permute-done((bf16[32,8,512]{2,1,0:T(8,128)(2,1)S(1)}, bf16[32,8,512]{2,1,0:T(8,128)(2,1)S(1)}, u32[]{:S(2)}, u32[]{:S(2)}) %collective-permute-start) | collective-permute-done | bytes 262176 | tf_op jit(solution)/shard_map/ppermute | solution.py:214
  17.8 0.1 shard_map.87.near_ref
  18.0 0.0 copy-start.2
  18.0 0.0 copy-start.3
  18.0 3.7 %collective-permute-done.3.far_a_ref = bf16[32,8,512]{2,1,0:T(8,128)(2,1)S(1)} collective-permute-done((bf16[32,8,512]{2,1,0:T(8,128)(2,1)S(1)}, bf16[32,8,512]{2,1,0:T(8,128)(2,1)S(1)}, u32[]{:S(2)}, u32[]{:S(2)}) %collective-permute-start.3) | collective-permute-done | bytes 262176 | tf_op jit(solution)/shard_map/ppermute | solution.py:214
  21.7 1.7 %collective-permute-done.5.far_b_ref = bf16[32,8,512]{2,1,0:T(8,128)(2,1)S(1)} collective-permute-done((bf16[32,8,512]{2,1,0:T(8,128)(2,1)S(1)}, bf16[32,8,512]{2,1,0:T(8,128)(2,1)S(1)}, u32[]{:S(2)}, u32[]{:S(2)}) %collective-permute-start.5) | collective-permute-done | bytes 262176 | tf_op jit(solution)/shard_map/ppermute | solution.py:214
  23.5 0.7 shard_map.90
  24.2 41.7 %all_to_all.10.held_ref = bf16[64,2,8,512]{3,2,1,0:T(8,128)(2,1)S(1)} all-to-all(bf16[64,2,8,512]{3,2,1,0:T(8,128)(2,1)S(1)} %bitcast.17), channel_id=1, replica_groups=mesh['rep'=4,'fsdp'=64] {'fsdp'}, dimensions={0} | all-to-all | bytes 2097152 | tf_op jit(solution)/shard_map/all_to_all | solution.py:234
  65.9 2.0 %shard_map.91 = bf16[64,2,8,512]{3,2,1,0:T(8,128)(2,1)} custom-call(bf16[64,2,8,512]{3,2,1,0:T(8,128)(2,1)S(1)} %all_to_all.10.held_ref, bf16[2,512,512]{2,1,0:T(8,128)(2,1)S(1)} %copy-done.2, bf16[2,512,512]{2,1,0:T(8,128)(2,1)S(1)} %copy-done.3), custom_call_target="tpu_custom_call" | custom-call | flops 1073741824 | bytes 4194304 | tf_op jit(solution)/shard_map/pallas_call | solution.py:133
  67.9 6.2 %all-to-all-start.1 = ((bf16[64,2,8,512]{3,2,1,0:T(8,128)(2,1)}), bf16[64,2,8,512]{3,2,1,0:T(8,128)(2,1)S(1)}, u32[]{:S(2)}, u32[]{:S(2)}) async-start(bf16[64,2,8,512]{3,2,1,0:T(8,128)(2,1)} %shard_map.91), calls=%async_computation.1 | async-start | bytes 2097152 | tf_op jit(solution)/shard_map/all_to_all | solution.py:236
  74.1 0.0 copy-start
  74.2 1.6 %copy-done = f32[2,512,512]{2,1,0:T(8,128)S(1)} copy-done((f32[2,512,512]{2,1,0:T(8,128)S(1)}, f32[2,512,512]{2,1,0:T(8,128)}, u32[]{:S(2)}) %copy-start) | copy-done | bytes 2097176
  75.7 1.6 %copy-done.1 = f32[2,512,512]{2,1,0:T(8,128)S(1)} copy-done((f32[2,512,512]{2,1,0:T(8,128)S(1)}, f32[2,512,512]{2,1,0:T(8,128)}, u32[]{:S(2)}) %copy-start.1) | copy-done | bytes 2097176
  77.3 2.7 %shard_map.93 = (f32[2,512,512]{2,1,0:T(8,128)}, f32[2,512,512]{2,1,0:T(8,128)}) custom-call(bf16[64,2,8,512]{3,2,1,0:T(8,128)(2,1)S(1)} %all_to_all.10.held_ref, f32[2,512,512]{2,1,0:T(8,128)S(1)} %copy-done, f32[2,512,512]{2,1,0:T(8,128)S(1)} %copy-done.1), custom_call_target="tpu_custom_call" | custom-call | flops 1073741824 | bytes 10485760 | tf_op jit(solution)/shard_map/pallas_call | solution.py:161
  80.0 22.7 %all-to-all-done.1 = bf16[64,2,8,512]{3,2,1,0:T(8,128)(2,1)S(1)} async-done(((bf16[64,2,8,512]{3,2,1,0:T(8,128)(2,1)}), bf16[64,2,8,512]{3,2,1,0:T(8,128)(2,1)S(1)}, u32[]{:S(2)}, u32[]{:S(2)}) %all-to-all-start.1) | async-done | bytes 1048608 | tf_op jit(solution)/shard_map/all_to_all | solution.py:236
  102.7 1.4 %shard_map.92 = bf16[64,8,512]{2,1,0:T(8,128)(2,1)} custom-call(s32[64]{0:T(128)S(1)} %multiply_add_fusion.place_ref, bf16[128,8,512]{2,1,0:T(8,128)(2,1)S(1)} %bitcast.16), custom_call_target="tpu_custom_call" | custom-call | bytes 2097152 | tf_op jit(solution)/shard_map/pallas_call | solution.py:193
  (8 shorter events, 0.0 us)
Async XLA Ops:
  1.7 11.6 %collective-permute-start.4 = (bf16[32,8,512]{2,1,0:T(8,128)(2,1)S(1)}, bf16[32,8,512]{2,1,0:T(8,128)(2,1)S(1)}, u32[]{:S(2)}, u32[]{:S(2)}) collective-permute-start(bf16[32,8,512]{2,1,0:T(8,128)(2,1)S(1)} %get-tuple-element.17), channel_id=1, source_target_pairs={{0,192},{64,128},{128,64},{192,0},{1,193},{65,129},{129,65},{193,1... | collective-permute-start | bytes 786440 | tf_op jit(solution)/shard_map/ppermute | solution.py:214
  5.4 6.9 %collective-permute-start.2 = (bf16[32,8,512]{2,1,0:T(8,128)(2,1)S(1)}, bf16[32,8,512]{2,1,0:T(8,128)(2,1)S(1)}, u32[]{:S(2)}, u32[]{:S(2)}) collective-permute-start(bf16[32,8,512]{2,1,0:T(8,128)(2,1)S(1)} %get-tuple-element.18), channel_id=1, source_target_pairs={{0,64},{64,0},{128,192},{192,128},{1,65},{65,1},{129,193},{193,129... | collective-permute-start | bytes 786440 | tf_op jit(solution)/shard_map/ppermute | solution.py:214
  5.4 5.1 %copy-start.4 = (s32[256,1]{0,1:T(1,128)S(1)}, s32[256,1]{0,1:T(1,128)}, u32[]{:S(2)}) copy-start(s32[256,1]{0,1:T(1,128)} %param.7) | copy-start | bytes 3076
  7.0 10.8 %collective-permute-start = (bf16[32,8,512]{2,1,0:T(8,128)(2,1)S(1)}, bf16[32,8,512]{2,1,0:T(8,128)(2,1)S(1)}, u32[]{:S(2)}, u32[]{:S(2)}) collective-permute-start(bf16[32,8,512]{2,1,0:T(8,128)(2,1)S(1)} %get-tuple-element.11), channel_id=1, source_target_pairs={{0,64},{64,0},{128,192},{192,128},{1,65},{65,1},{129,193},{193,129... | collective-permute-start | bytes 786440 | tf_op jit(solution)/shard_map/ppermute | solution.py:214
  8.6 9.2 %collective-permute-start.1 = (bf16[32,8,512]{2,1,0:T(8,128)(2,1)S(1)}, bf16[32,8,512]{2,1,0:T(8,128)(2,1)S(1)}, u32[]{:S(2)}, u32[]{:S(2)}) collective-permute-start(bf16[32,8,512]{2,1,0:T(8,128)(2,1)S(1)} %get-tuple-element.12), channel_id=1, source_target_pairs={{0,192},{64,128},{128,64},{192,0},{1,193},{65,129},{129,65},{193,1... | collective-permute-start | bytes 786440 | tf_op jit(solution)/shard_map/ppermute | solution.py:214
  12.3 9.4 %collective-permute-start.3 = (bf16[32,8,512]{2,1,0:T(8,128)(2,1)S(1)}, bf16[32,8,512]{2,1,0:T(8,128)(2,1)S(1)}, u32[]{:S(2)}, u32[]{:S(2)}) collective-permute-start(bf16[32,8,512]{2,1,0:T(8,128)(2,1)S(1)} %shard_map.88), channel_id=1, source_target_pairs={{0,192},{64,128},{128,64},{192,0},{1,193},{65,129},{129,65},{193,1... | collective-permute-start | bytes 786440 | tf_op jit(solution)/shard_map/ppermute | solution.py:214
  13.4 10.0 %collective-permute-start.5 = (bf16[32,8,512]{2,1,0:T(8,128)(2,1)S(1)}, bf16[32,8,512]{2,1,0:T(8,128)(2,1)S(1)}, u32[]{:S(2)}, u32[]{:S(2)}) collective-permute-start(bf16[32,8,512]{2,1,0:T(8,128)(2,1)S(1)} %shard_map.89), channel_id=1, source_target_pairs={{0,64},{64,0},{128,192},{192,128},{1,65},{65,1},{129,193},{193,129... | collective-permute-start | bytes 786440 | tf_op jit(solution)/shard_map/ppermute | solution.py:214
  18.0 47.9 %copy-start.2 = (bf16[2,512,512]{2,1,0:T(8,128)(2,1)S(1)}, bf16[2,512,512]{2,1,0:T(8,128)(2,1)}, u32[]{:S(2)}) copy-start(bf16[2,512,512]{2,1,0:T(8,128)(2,1)} %left_ref.2) | copy-start | bytes 3145732
  18.0 47.9 %copy-start.3 = (bf16[2,512,512]{2,1,0:T(8,128)(2,1)S(1)}, bf16[2,512,512]{2,1,0:T(8,128)(2,1)}, u32[]{:S(2)}) copy-start(bf16[2,512,512]{2,1,0:T(8,128)(2,1)} %right_ref.2) | copy-start | bytes 3145732
  67.9 34.8 %all-to-all-start.1 = ((bf16[64,2,8,512]{3,2,1,0:T(8,128)(2,1)}), bf16[64,2,8,512]{3,2,1,0:T(8,128)(2,1)S(1)}, u32[]{:S(2)}, u32[]{:S(2)}) async-start(bf16[64,2,8,512]{3,2,1,0:T(8,128)(2,1)} %shard_map.91), calls=%async_computation.1 | async-start | bytes 2097152 | tf_op jit(solution)/shard_map/all_to_all | solution.py:236
  74.1 1.6 %copy-start = (f32[2,512,512]{2,1,0:T(8,128)S(1)}, f32[2,512,512]{2,1,0:T(8,128)}, u32[]{:S(2)}) copy-start(f32[2,512,512]{2,1,0:T(8,128)} %left_ref.3) | copy-start | bytes 6291460
  75.7 1.6 %copy-start.1 = (f32[2,512,512]{2,1,0:T(8,128)S(1)}, f32[2,512,512]{2,1,0:T(8,128)}, u32[]{:S(2)}) copy-start(f32[2,512,512]{2,1,0:T(8,128)} %right_ref.3) | copy-start | bytes 6291460

commit v5 on v4

--- a/solution.py
+++ b/solution.py
@@ -66,46 +66,50 @@
     )(a, b)
 
 
-def near_kernel(own_ref, near_a_ref, near_b_ref, sum_ref):
+def near_kernel(own_ref, near_a_ref, near_b_ref, sum_ref, empty_ref):
+    empty_ref[...] = jnp.zeros_like(empty_ref)
     half = near_a_ref.shape[0]
     sum_ref[:half] = wide(own_ref[:half]) + wide(near_a_ref[...])
     sum_ref[half:] = wide(own_ref[half:]) + wide(near_b_ref[...])
 
 
-def near_sum(own, near_a, near_b):
+def near_sum(own, near_a, near_b, place_count):
     return pl.pallas_call(
         near_kernel,
         in_specs=[IN_VMEM] * 3,
-        out_specs=IN_VMEM,
-        out_shape=pltpu.VMEM(own.shape, jnp.float32),
+        out_specs=[IN_VMEM] * 2,
+        out_shape=[
+            pltpu.VMEM(own.shape, jnp.float32),
+            pltpu.VMEM((place_count,) + own.shape[1:], own.dtype),
+        ],
         compiler_params=pltpu.CompilerParams(vmem_limit_bytes=8 * MIB),
         cost_estimate=pl.CostEstimate(flops=own.size, bytes_accessed=2 * MIB, transcendentals=0),
     )(own, near_a, near_b)
 
 
-def place_kernel(place_ref, near_ref, far_a_ref, far_b_ref, out_ref):
-    out_ref[...] = jnp.zeros_like(out_ref)
-    half = far_a_ref.shape[0]
-
-    def step(i, carry):
-        for k, far in ((i, far_a_ref), (i + half, far_b_ref)):
-            total = near_ref[k] + wide(far[i])
-            out_ref[place_ref[k]] = total.astype(jnp.bfloat16)
-        return carry
-
-    lax.fori_loop(0, half, step, 0, unroll=8)
-
-
-def place(places, near, far_a, far_b, place_count):
-    shape = (place_count,) + near.shape[1:]
+def place_kernel(place_ref, near_ref, far_a_ref, far_b_ref, empty_ref, out_ref):
+    del empty_ref
+    share = far_a_ref.shape[0]
+    for first, far_ref in ((0, far_a_ref), (share, far_b_ref)):
+
+        def step(i, carry, first=first, far_ref=far_ref):
+            total = near_ref[first + i] + wide(far_ref[i])
+            out_ref[place_ref[first + i]] = total.astype(jnp.bfloat16)
+            return carry
+
+        lax.fori_loop(0, share, step, 0, unroll=share)
+
+
+def place(places, near, far_a, far_b, empty):
     return pl.pallas_call(
         place_kernel,
-        in_specs=[IN_SMEM] + [IN_VMEM] * 3,
+        in_specs=[IN_SMEM] + [IN_VMEM] * 4,
         out_specs=IN_VMEM,
-        out_shape=jax.ShapeDtypeStruct(shape, jnp.bfloat16),
+        out_shape=jax.ShapeDtypeStruct(empty.shape, jnp.bfloat16),
+        input_output_aliases={4: 0},
         compiler_params=pltpu.CompilerParams(vmem_limit_bytes=8 * MIB),
         cost_estimate=pl.CostEstimate(flops=near.size, bytes_accessed=3 * MIB, transcendentals=0),
-    )(places, near, far_a, far_b)
+    )(places, near, far_a, far_b, empty)
 
 
 def product_kernel(held_ref, left_ref, right_ref, update_ref, made, sems):
@@ -228,8 +232,8 @@
     far_a, far_b = swap(on_a, 3), swap(on_b, 1)
 
     places = my_places(block_owners, quarter, per_quarter, slot_count)
-    near = near_sum(own, near_a, near_b)
-    placed = place(places, near, far_a, far_b, owner_count * slot_count)
+    near, empty = near_sum(own, near_a, near_b, owner_count * slot_count)
+    placed = place(places, near, far_a, far_b, empty)
     placed = placed.reshape((owner_count, slot_count) + placed.shape[1:])
     held = lax.all_to_all(placed, "fsdp", split_axis=0, concat_axis=0, tiled=True)
     update_slots = products(held, left_roots, right_roots)

time: 104 us -> 104 us (level)
  no operation moved by 1% of the time
where the time goes in v5:
time: 104 us
  blocking collectives  41.7 us (40%)
  waiting for transfers between devices  33.8 us (32%)
  starting transfers between devices  12.7 us (12%)
  Pallas kernels  10.3 us (10%)
  local copies, waits for them, and re-layouts  4.34 us (4%)
    all_to_all x1, blocking collectives, on_device(): lax.all_to_all(placed, 'fsdp', split_axis=0, concat_axis=0, tiled=True)  41.7 us
    all_to_all x1, waiting for transfers between devices, on_device(): lax.all_to_all(update_slots, 'fsdp', split_axis=0, concat_axis=0, tiled=T...  22.7 us
    ppermute x6, waiting for transfers between devices, swap(): return lax.ppermute(value, 'rep', [(i, i ^ bit) for i in range(rep_count)])  11.1 us
    ppermute x6, starting transfers between devices, swap(): return lax.ppermute(value, 'rep', [(i, i ^ bit) for i in range(rep_count)])  6.46 us
    all_to_all x1, starting transfers between devices, on_device(): lax.all_to_all(update_slots, 'fsdp', split_axis=0, concat_axis=0, tiled=T...  6.2 us
    pallas_call x2, Pallas kernels, cut(): pl.pallas_call(cut_kernel, in_specs=[IN_SMEM, IN_HBM], out_specs=[IN_VMEM...  3.35 us
    unnamed x10, local copies, waits for them, and re-layouts  3.19 us
    pallas_call x1, Pallas kernels, statistics(): pl.pallas_call(stats_kernel, grid=(slot_count,), in_specs=[pl.BlockSpec((...  2.64 us
  transfers between devices with their start and end apart: 7, of which 5 were waited for; matrix products, arithmetic and copies ran while one was open for 0% of the time, Pallas kernels for 6%

profile of v5, /device:TPU:1, one launch (start us, length us, event | category | flops | bytes accessed | tf_op | source)
XLA Modules:
  0.0 104.0 jit_solution(2327070756295787342)
XLA Ops:
  0.6 1.1 %dynamic-slice_bitcast_fusion = (bf16[32,8,512]{2,1,0:T(8,128)(2,1)S(1)}, bf16[32,8,512]{2,1,0:T(8,128)(2,1)S(1)}) fusion(bf16[1,256,8,512]{3,2,1,0:T(8,128)(2,1)} %param.6, s32[]{:T(128)S(6)} %select_n.11, s32[]{:T(128)S(6)} %select_n.10), kind=kLoop, calls=%fused_computation | loop fusion | bytes 1048584 | tf_op jit(solution)/shard_map/dynamic_slice | solution.py:224
  1.7 3.7 %collective-permute-start.4 = (bf16[32,8,512]{2,1,0:T(8,128)(2,1)S(1)}, bf16[32,8,512]{2,1,0:T(8,128)(2,1)S(1)}, u32[]{:S(2)}, u32[]{:S(2)}) collective-permute-start(bf16[32,8,512]{2,1,0:T(8,128)(2,1)S(1)} %get-tuple-element.21), channel_id=1, source_target_pairs={{0,192},{64,128},{128,64},{192,0},{1,193},{65,129},{129,65},{193,1... | collective-permute-start | bytes 786440 | tf_op jit(solution)/shard_map/ppermute | solution.py:218
  5.4 0.1 pad_add_fusion.1.starts_ref
  5.4 1.6 %shard_map.86 = (bf16[32,8,512]{2,1,0:T(8,128)(2,1)S(1)}, bf16[32,8,512]{2,1,0:T(8,128)(2,1)S(1)}) custom-call(s32[2]{0:T(128)S(1)} %pad_add_fusion.1.starts_ref, bf16[256,8,512]{2,1,0:T(8,128)(2,1)} %bitcast.18), custom_call_target="tpu_custom_call" | custom-call | bytes 2097152 | tf_op jit(solution)/shard_map/pallas_call | solution.py:43
  7.0 1.5 %collective-permute-start = (bf16[32,8,512]{2,1,0:T(8,128)(2,1)S(1)}, bf16[32,8,512]{2,1,0:T(8,128)(2,1)S(1)}, u32[]{:S(2)}, u32[]{:S(2)}) collective-permute-start(bf16[32,8,512]{2,1,0:T(8,128)(2,1)S(1)} %get-tuple-element.13), channel_id=1, source_target_pairs={{0,64},{64,0},{128,192},{192,128},{1,65},{65,1},{129,193},{193,129... | collective-permute-start | bytes 786440 | tf_op jit(solution)/shard_map/ppermute | solution.py:218
  8.6 0.1 collective-permute-start.1
  8.7 0.1 pad_add_fusion.starts_ref
  8.8 1.8 %shard_map.85 = (bf16[64,8,512]{2,1,0:T(8,128)(2,1)S(1)}, bf16[32,8,512]{2,1,0:T(8,128)(2,1)S(1)}, bf16[32,8,512]{2,1,0:T(8,128)(2,1)S(1)}) custom-call(s32[3]{0:T(128)S(1)} %pad_add_fusion.starts_ref, bf16[256,8,512]{2,1,0:T(8,128)(2,1)} %bitcast.19), custom_call_target="tpu_custom_call" | custom-call | bytes 2097152 | tf_op jit(solution)/shard_map/pallas_call | solution.py:43
  10.5 0.1 fusion.1
  10.6 1.6 %collective-permute-done.2.b_ref = bf16[32,8,512]{2,1,0:T(8,128)(2,1)S(1)} collective-permute-done((bf16[32,8,512]{2,1,0:T(8,128)(2,1)S(1)}, bf16[32,8,512]{2,1,0:T(8,128)(2,1)S(1)}, u32[]{:S(2)}, u32[]{:S(2)}) %collective-permute-start.2) | collective-permute-done | bytes 262176 | tf_op jit(solution)/shard_map/ppermute | solution.py:218
  12.2 0.1 shard_map.88
  12.3 1.1 %collective-permute-start.3 = (bf16[32,8,512]{2,1,0:T(8,128)(2,1)S(1)}, bf16[32,8,512]{2,1,0:T(8,128)(2,1)S(1)}, u32[]{:S(2)}, u32[]{:S(2)}) collective-permute-start(bf16[32,8,512]{2,1,0:T(8,128)(2,1)S(1)} %shard_map.88), channel_id=1, source_target_pairs={{0,192},{64,128},{128,64},{192,0},{1,193},{65,129},{129,65},{193,1... | collective-permute-start | bytes 786440 | tf_op jit(solution)/shard_map/ppermute | solution.py:218
  13.4 0.0 collective-permute-done.4.b_ref
  13.4 0.1 shard_map.89
  13.4 0.1 collective-permute-start.5
  13.5 0.2 convert_reduce_fusion
  13.7 0.1 multiply_add_fusion.place_ref
  13.8 4.1 %collective-permute-done.near_a_ref = bf16[32,8,512]{2,1,0:T(8,128)(2,1)S(1)} collective-permute-done((bf16[32,8,512]{2,1,0:T(8,128)(2,1)S(1)}, bf16[32,8,512]{2,1,0:T(8,128)(2,1)S(1)}, u32[]{:S(2)}, u32[]{:S(2)}) %collective-permute-start) | collective-permute-done | bytes 262176 | tf_op jit(solution)/shard_map/ppermute | solution.py:218
  17.8 0.0 collective-permute-done.1.near_b_ref
  17.8 0.2 shard_map.87
  18.0 3.7 %collective-permute-done.3.far_a_ref = bf16[32,8,512]{2,1,0:T(8,128)(2,1)S(1)} collective-permute-done((bf16[32,8,512]{2,1,0:T(8,128)(2,1)S(1)}, bf16[32,8,512]{2,1,0:T(8,128)(2,1)S(1)}, u32[]{:S(2)}, u32[]{:S(2)}) %collective-permute-start.3) | collective-permute-done | bytes 262176 | tf_op jit(solution)/shard_map/ppermute | solution.py:218
  21.7 1.7 %collective-permute-done.5.far_b_ref = bf16[32,8,512]{2,1,0:T(8,128)(2,1)S(1)} collective-permute-done((bf16[32,8,512]{2,1,0:T(8,128)(2,1)S(1)}, bf16[32,8,512]{2,1,0:T(8,128)(2,1)S(1)}, u32[]{:S(2)}, u32[]{:S(2)}) %collective-permute-start.5) | collective-permute-done | bytes 262176 | tf_op jit(solution)/shard_map/ppermute | solution.py:218
  23.5 0.6 shard_map.90
  24.1 41.7 %all_to_all.10.held_ref = bf16[64,2,8,512]{3,2,1,0:T(8,128)(2,1)S(1)} all-to-all(bf16[64,2,8,512]{3,2,1,0:T(8,128)(2,1)S(1)} %bitcast.17), channel_id=1, replica_groups=mesh['rep'=4,'fsdp'=64] {'fsdp'}, dimensions={0} | all-to-all | bytes 2097152 | tf_op jit(solution)/shard_map/all_to_all | solution.py:238
  65.8 2.0 %shard_map.91 = bf16[64,2,8,512]{3,2,1,0:T(8,128)(2,1)} custom-call(bf16[64,2,8,512]{3,2,1,0:T(8,128)(2,1)S(1)} %all_to_all.10.held_ref, bf16[2,512,512]{2,1,0:T(8,128)(2,1)S(1)} %copy-done.2, bf16[2,512,512]{2,1,0:T(8,128)(2,1)S(1)} %copy-done.3), custom_call_target="tpu_custom_call" | custom-call | flops 1073741824 | bytes 4194304 | tf_op jit(solution)/shard_map/pallas_call | solution.py:137
  67.8 6.2 %all-to-all-start.1 = ((bf16[64,2,8,512]{3,2,1,0:T(8,128)(2,1)}), bf16[64,2,8,512]{3,2,1,0:T(8,128)(2,1)S(1)}, u32[]{:S(2)}, u32[]{:S(2)}) async-start(bf16[64,2,8,512]{3,2,1,0:T(8,128)(2,1)} %shard_map.91), calls=%async_computation.1 | async-start | bytes 2097152 | tf_op jit(solution)/shard_map/all_to_all | solution.py:240
  74.1 0.0 copy-start
  74.1 1.6 %copy-done = f32[2,512,512]{2,1,0:T(8,128)S(1)} copy-done((f32[2,512,512]{2,1,0:T(8,128)S(1)}, f32[2,512,512]{2,1,0:T(8,128)}, u32[]{:S(2)}) %copy-start) | copy-done | bytes 2097176
  75.6 1.6 %copy-done.1 = f32[2,512,512]{2,1,0:T(8,128)S(1)} copy-done((f32[2,512,512]{2,1,0:T(8,128)S(1)}, f32[2,512,512]{2,1,0:T(8,128)}, u32[]{:S(2)}) %copy-start.1) | copy-done | bytes 2097176
  77.2 2.6 %shard_map.93 = (f32[2,512,512]{2,1,0:T(8,128)}, f32[2,512,512]{2,1,0:T(8,128)}) custom-call(bf16[64,2,8,512]{3,2,1,0:T(8,128)(2,1)S(1)} %all_to_all.10.held_ref, f32[2,512,512]{2,1,0:T(8,128)S(1)} %copy-done, f32[2,512,512]{2,1,0:T(8,128)S(1)} %copy-done.1), custom_call_target="tpu_custom_call" | custom-call | flops 1073741824 | bytes 10485760 | tf_op jit(solution)/shard_map/pallas_call | solution.py:165
  79.9 22.7 %all-to-all-done.1 = bf16[64,2,8,512]{3,2,1,0:T(8,128)(2,1)S(1)} async-done(((bf16[64,2,8,512]{3,2,1,0:T(8,128)(2,1)}), bf16[64,2,8,512]{3,2,1,0:T(8,128)(2,1)S(1)}, u32[]{:S(2)}, u32[]{:S(2)}) %all-to-all-start.1) | async-done | bytes 1048608 | tf_op jit(solution)/shard_map/all_to_all | solution.py:240
  102.6 1.4 %shard_map.92 = bf16[64,8,512]{2,1,0:T(8,128)(2,1)} custom-call(s32[64]{0:T(128)S(1)} %multiply_add_fusion.place_ref, bf16[128,8,512]{2,1,0:T(8,128)(2,1)S(1)} %bitcast.16), custom_call_target="tpu_custom_call" | custom-call | bytes 2097152 | tf_op jit(solution)/shard_map/pallas_call | solution.py:197
  (8 shorter events, 0.0 us)
Async XLA Ops:
  1.7 11.6 %collective-permute-start.4 = (bf16[32,8,512]{2,1,0:T(8,128)(2,1)S(1)}, bf16[32,8,512]{2,1,0:T(8,128)(2,1)S(1)}, u32[]{:S(2)}, u32[]{:S(2)}) collective-permute-start(bf16[32,8,512]{2,1,0:T(8,128)(2,1)S(1)} %get-tuple-element.21), channel_id=1, source_target_pairs={{0,192},{64,128},{128,64},{192,0},{1,193},{65,129},{129,65},{193,1... | collective-permute-start | bytes 786440 | tf_op jit(solution)/shard_map/ppermute | solution.py:218
  5.4 6.9 %collective-permute-start.2 = (bf16[32,8,512]{2,1,0:T(8,128)(2,1)S(1)}, bf16[32,8,512]{2,1,0:T(8,128)(2,1)S(1)}, u32[]{:S(2)}, u32[]{:S(2)}) collective-permute-start(bf16[32,8,512]{2,1,0:T(8,128)(2,1)S(1)} %get-tuple-element.22), channel_id=1, source_target_pairs={{0,64},{64,0},{128,192},{192,128},{1,65},{65,1},{129,193},{193,129... | collective-permute-start | bytes 786440 | tf_op jit(solution)/shard_map/ppermute | solution.py:218
  5.4 5.1 %copy-start.4 = (s32[256,1]{0,1:T(1,128)S(1)}, s32[256,1]{0,1:T(1,128)}, u32[]{:S(2)}) copy-start(s32[256,1]{0,1:T(1,128)} %param.7) | copy-start | bytes 3076
  7.0 10.8 %collective-permute-start = (bf16[32,8,512]{2,1,0:T(8,128)(2,1)S(1)}, bf16[32,8,512]{2,1,0:T(8,128)(2,1)S(1)}, u32[]{:S(2)}, u32[]{:S(2)}) collective-permute-start(bf16[32,8,512]{2,1,0:T(8,128)(2,1)S(1)} %get-tuple-element.13), channel_id=1, source_target_pairs={{0,64},{64,0},{128,192},{192,128},{1,65},{65,1},{129,193},{193,129... | collective-permute-start | bytes 786440 | tf_op jit(solution)/shard_map/ppermute | solution.py:218
  8.6 9.2 %collective-permute-start.1 = (bf16[32,8,512]{2,1,0:T(8,128)(2,1)S(1)}, bf16[32,8,512]{2,1,0:T(8,128)(2,1)S(1)}, u32[]{:S(2)}, u32[]{:S(2)}) collective-permute-start(bf16[32,8,512]{2,1,0:T(8,128)(2,1)S(1)} %get-tuple-element.14), channel_id=1, source_target_pairs={{0,192},{64,128},{128,64},{192,0},{1,193},{65,129},{129,65},{193,1... | collective-permute-start | bytes 786440 | tf_op jit(solution)/shard_map/ppermute | solution.py:218
  12.3 9.4 %collective-permute-start.3 = (bf16[32,8,512]{2,1,0:T(8,128)(2,1)S(1)}, bf16[32,8,512]{2,1,0:T(8,128)(2,1)S(1)}, u32[]{:S(2)}, u32[]{:S(2)}) collective-permute-start(bf16[32,8,512]{2,1,0:T(8,128)(2,1)S(1)} %shard_map.88), channel_id=1, source_target_pairs={{0,192},{64,128},{128,64},{192,0},{1,193},{65,129},{129,65},{193,1... | collective-permute-start | bytes 786440 | tf_op jit(solution)/shard_map/ppermute | solution.py:218
  13.4 10.0 %collective-permute-start.5 = (bf16[32,8,512]{2,1,0:T(8,128)(2,1)S(1)}, bf16[32,8,512]{2,1,0:T(8,128)(2,1)S(1)}, u32[]{:S(2)}, u32[]{:S(2)}) collective-permute-start(bf16[32,8,512]{2,1,0:T(8,128)(2,1)S(1)} %shard_map.89), channel_id=1, source_target_pairs={{0,64},{64,0},{128,192},{192,128},{1,65},{65,1},{129,193},{193,129... | collective-permute-start | bytes 786440 | tf_op jit(solution)/shard_map/ppermute | solution.py:218
  23.5 42.3 %copy-start.2 = (bf16[2,512,512]{2,1,0:T(8,128)(2,1)S(1)}, bf16[2,512,512]{2,1,0:T(8,128)(2,1)}, u32[]{:S(2)}) copy-start(bf16[2,512,512]{2,1,0:T(8,128)(2,1)} %left_ref.2) | copy-start | bytes 3145732
  23.5 42.3 %copy-start.3 = (bf16[2,512,512]{2,1,0:T(8,128)(2,1)S(1)}, bf16[2,512,512]{2,1,0:T(8,128)(2,1)}, u32[]{:S(2)}) copy-start(bf16[2,512,512]{2,1,0:T(8,128)(2,1)} %right_ref.2) | copy-start | bytes 3145732
  67.8 34.8 %all-to-all-start.1 = ((bf16[64,2,8,512]{3,2,1,0:T(8,128)(2,1)}), bf16[64,2,8,512]{3,2,1,0:T(8,128)(2,1)S(1)}, u32[]{:S(2)}, u32[]{:S(2)}) async-start(bf16[64,2,8,512]{3,2,1,0:T(8,128)(2,1)} %shard_map.91), calls=%async_computation.1 | async-start | bytes 2097152 | tf_op jit(solution)/shard_map/all_to_all | solution.py:240
  74.1 1.6 %copy-start = (f32[2,512,512]{2,1,0:T(8,128)S(1)}, f32[2,512,512]{2,1,0:T(8,128)}, u32[]{:S(2)}) copy-start(f32[2,512,512]{2,1,0:T(8,128)} %left_ref.3) | copy-start | bytes 6291460
  75.6 1.6 %copy-start.1 = (f32[2,512,512]{2,1,0:T(8,128)S(1)}, f32[2,512,512]{2,1,0:T(8,128)}, u32[]{:S(2)}) copy-start(f32[2,512,512]{2,1,0:T(8,128)} %right_ref.3) | copy-start | bytes 6291460

commit v6 on v5

--- a/solution.py
+++ b/solution.py
@@ -170,7 +170,11 @@
         out_shape=[jax.ShapeDtypeStruct(left_stats.shape, jnp.float32)] * 2,
         compiler_params=pltpu.CompilerParams(vmem_limit_bytes=24 * MIB),
         cost_estimate=pl.CostEstimate(flops=2**30, bytes_accessed=10 * MIB, transcendentals=0),
-    )(held, left_stats, right_stats)
+    )(
+        held,
+        pltpu.with_memory_space_constraint(left_stats, pltpu.HBM),
+        pltpu.with_memory_space_constraint(right_stats, pltpu.HBM),
+    )
 
 
 def take_kernel(place_ref, held_ref, out_ref, gathered, sems):

time: 104 us -> 104 us (level)
  local copies, waits for them, and re-layouts: 4.34 us -> 1.16 us
  waiting for transfers between devices: 33.8 us -> 35.5 us
  Pallas kernels: 10.3 us -> 11.8 us
    unnamed x10 -> x6, local copies, waits for them, and re-layouts: 3.19 us -> 0.01 us
    all_to_all x1, waiting for transfers between devices: 22.7 us -> 24.4 us  [on_device(): lax.all_to_all(update_slots, 'fsdp', split_axis=0, concat_axis=0, tiled=T...]
    pallas_call x1, Pallas kernels: 2.64 us -> 4.16 us  [statistics(): pl.pallas_call(stats_kernel, grid=(slot_count,), in_specs=[pl.BlockSpec((...]
  transfers between devices with their start and end apart: 7 -> 7, of which waited for: 5 -> 5; matrix products, arithmetic and copies ran while one was open for 0% -> 0% of each run, Pallas kernels for 6% -> 7%
where the time goes in v6:
time: 104 us
  blocking collectives  41.7 us (40%)
  waiting for transfers between devices  35.5 us (34%)
  starting transfers between devices  12.7 us (12%)
  Pallas kernels  11.8 us (11%)
  local copies, waits for them, and re-layouts  1.16 us (1%)
    all_to_all x1, blocking collectives, on_device(): lax.all_to_all(placed, 'fsdp', split_axis=0, concat_axis=0, tiled=True)  41.7 us
    all_to_all x1, waiting for transfers between devices, on_device(): lax.all_to_all(update_slots, 'fsdp', split_axis=0, concat_axis=0, tiled=T...  24.4 us
    ppermute x6, waiting for transfers between devices, swap(): return lax.ppermute(value, 'rep', [(i, i ^ bit) for i in range(rep_count)])  11.1 us
    ppermute x6, starting transfers between devices, swap(): return lax.ppermute(value, 'rep', [(i, i ^ bit) for i in range(rep_count)])  6.46 us
    all_to_all x1, starting transfers between devices, on_device(): lax.all_to_all(update_slots, 'fsdp', split_axis=0, concat_axis=0, tiled=T...  6.2 us
    pallas_call x1, Pallas kernels, statistics(): pl.pallas_call(stats_kernel, grid=(slot_count,), in_specs=[pl.BlockSpec((...  4.16 us
    pallas_call x2, Pallas kernels, cut(): pl.pallas_call(cut_kernel, in_specs=[IN_SMEM, IN_HBM], out_specs=[IN_VMEM...  3.35 us
  transfers between devices with their start and end apart: 7, of which 5 were waited for; matrix products, arithmetic and copies ran while one was open for 0% of the time, Pallas kernels for 7%

profile of v6, /device:TPU:1, one launch (start us, length us, event | category | flops | bytes accessed | tf_op | source)
XLA Modules:
  0.0 104.0 jit_solution(979952606920455319)
XLA Ops:
  0.6 1.1 %dynamic-slice_bitcast_fusion = (bf16[32,8,512]{2,1,0:T(8,128)(2,1)S(1)}, bf16[32,8,512]{2,1,0:T(8,128)(2,1)S(1)}) fusion(bf16[1,256,8,512]{3,2,1,0:T(8,128)(2,1)} %param.6, s32[]{:T(128)S(6)} %select_n.11, s32[]{:T(128)S(6)} %select_n.10), kind=kLoop, calls=%fused_computation | loop fusion | bytes 1048584 | tf_op jit(solution)/shard_map/dynamic_slice | solution.py:228
  1.7 3.7 %collective-permute-start.4 = (bf16[32,8,512]{2,1,0:T(8,128)(2,1)S(1)}, bf16[32,8,512]{2,1,0:T(8,128)(2,1)S(1)}, u32[]{:S(2)}, u32[]{:S(2)}) collective-permute-start(bf16[32,8,512]{2,1,0:T(8,128)(2,1)S(1)} %get-tuple-element.21), channel_id=1, source_target_pairs={{0,192},{64,128},{128,64},{192,0},{1,193},{65,129},{129,65},{193,1... | collective-permute-start | bytes 786440 | tf_op jit(solution)/shard_map/ppermute | solution.py:222
  5.4 0.0 collective-permute-start.2
  5.4 0.1 pad_add_fusion.1.starts_ref
  5.4 1.6 %shard_map.86 = (bf16[32,8,512]{2,1,0:T(8,128)(2,1)S(1)}, bf16[32,8,512]{2,1,0:T(8,128)(2,1)S(1)}) custom-call(s32[2]{0:T(128)S(1)} %pad_add_fusion.1.starts_ref, bf16[256,8,512]{2,1,0:T(8,128)(2,1)} %bitcast.18), custom_call_target="tpu_custom_call" | custom-call | bytes 2097152 | tf_op jit(solution)/shard_map/pallas_call | solution.py:43
  7.0 1.5 %collective-permute-start = (bf16[32,8,512]{2,1,0:T(8,128)(2,1)S(1)}, bf16[32,8,512]{2,1,0:T(8,128)(2,1)S(1)}, u32[]{:S(2)}, u32[]{:S(2)}) collective-permute-start(bf16[32,8,512]{2,1,0:T(8,128)(2,1)S(1)} %get-tuple-element.13), channel_id=1, source_target_pairs={{0,64},{64,0},{128,192},{192,128},{1,65},{65,1},{129,193},{193,129... | collective-permute-start | bytes 786440 | tf_op jit(solution)/shard_map/ppermute | solution.py:222
  8.6 0.1 collective-permute-start.1
  8.7 0.1 pad_add_fusion.starts_ref
  8.8 1.8 %shard_map.85 = (bf16[64,8,512]{2,1,0:T(8,128)(2,1)S(1)}, bf16[32,8,512]{2,1,0:T(8,128)(2,1)S(1)}, bf16[32,8,512]{2,1,0:T(8,128)(2,1)S(1)}) custom-call(s32[3]{0:T(128)S(1)} %pad_add_fusion.starts_ref, bf16[256,8,512]{2,1,0:T(8,128)(2,1)} %bitcast.19), custom_call_target="tpu_custom_call" | custom-call | bytes 2097152 | tf_op jit(solution)/shard_map/pallas_call | solution.py:43
  10.5 0.0 copy-done.2
  10.5 0.1 fusion.1
  10.6 1.6 %collective-permute-done.2.b_ref = bf16[32,8,512]{2,1,0:T(8,128)(2,1)S(1)} collective-permute-done((bf16[32,8,512]{2,1,0:T(8,128)(2,1)S(1)}, bf16[32,8,512]{2,1,0:T(8,128)(2,1)S(1)}, u32[]{:S(2)}, u32[]{:S(2)}) %collective-permute-start.2) | collective-permute-done | bytes 262176 | tf_op jit(solution)/shard_map/ppermute | solution.py:222
  12.2 0.1 shard_map.88
  12.3 1.1 %collective-permute-start.3 = (bf16[32,8,512]{2,1,0:T(8,128)(2,1)S(1)}, bf16[32,8,512]{2,1,0:T(8,128)(2,1)S(1)}, u32[]{:S(2)}, u32[]{:S(2)}) collective-permute-start(bf16[32,8,512]{2,1,0:T(8,128)(2,1)S(1)} %shard_map.88), channel_id=1, source_target_pairs={{0,192},{64,128},{128,64},{192,0},{1,193},{65,129},{129,65},{193,1... | collective-permute-start | bytes 786440 | tf_op jit(solution)/shard_map/ppermute | solution.py:222
  13.4 0.0 collective-permute-done.4.b_ref
  13.4 0.1 shard_map.89
  13.4 0.1 collective-permute-start.5
  13.5 0.2 convert_reduce_fusion
  13.7 0.1 multiply_add_fusion.place_ref
  13.8 4.1 %collective-permute-done.near_a_ref = bf16[32,8,512]{2,1,0:T(8,128)(2,1)S(1)} collective-permute-done((bf16[32,8,512]{2,1,0:T(8,128)(2,1)S(1)}, bf16[32,8,512]{2,1,0:T(8,128)(2,1)S(1)}, u32[]{:S(2)}, u32[]{:S(2)}) %collective-permute-start) | collective-permute-done | bytes 262176 | tf_op jit(solution)/shard_map/ppermute | solution.py:222
  17.8 0.0 collective-permute-done.1.near_b_ref
  17.8 0.2 shard_map.87
  18.0 3.7 %collective-permute-done.3.far_a_ref = bf16[32,8,512]{2,1,0:T(8,128)(2,1)S(1)} collective-permute-done((bf16[32,8,512]{2,1,0:T(8,128)(2,1)S(1)}, bf16[32,8,512]{2,1,0:T(8,128)(2,1)S(1)}, u32[]{:S(2)}, u32[]{:S(2)}) %collective-permute-start.3) | collective-permute-done | bytes 262176 | tf_op jit(solution)/shard_map/ppermute | solution.py:222
  21.7 1.7 %collective-permute-done.5.far_b_ref = bf16[32,8,512]{2,1,0:T(8,128)(2,1)S(1)} collective-permute-done((bf16[32,8,512]{2,1,0:T(8,128)(2,1)S(1)}, bf16[32,8,512]{2,1,0:T(8,128)(2,1)S(1)}, u32[]{:S(2)}, u32[]{:S(2)}) %collective-permute-start.5) | collective-permute-done | bytes 262176 | tf_op jit(solution)/shard_map/ppermute | solution.py:222
  23.5 0.6 shard_map.90
  24.1 41.7 %all_to_all.10.held_ref = bf16[64,2,8,512]{3,2,1,0:T(8,128)(2,1)S(1)} all-to-all(bf16[64,2,8,512]{3,2,1,0:T(8,128)(2,1)S(1)} %bitcast.17), channel_id=1, replica_groups=mesh['rep'=4,'fsdp'=64] {'fsdp'}, dimensions={0} | all-to-all | bytes 2097152 | tf_op jit(solution)/shard_map/all_to_all | solution.py:242
  65.8 0.0 copy-done.1
  65.8 2.0 %shard_map.91 = bf16[64,2,8,512]{3,2,1,0:T(8,128)(2,1)} custom-call(bf16[64,2,8,512]{3,2,1,0:T(8,128)(2,1)S(1)} %all_to_all.10.held_ref, bf16[2,512,512]{2,1,0:T(8,128)(2,1)S(1)} %copy-done, bf16[2,512,512]{2,1,0:T(8,128)(2,1)S(1)} %copy-done.1), custom_call_target="tpu_custom_call" | custom-call | flops 1073741824 | bytes 4194304 | tf_op jit(solution)/shard_map/pallas_call | solution.py:137
  67.8 6.2 %all-to-all-start.1 = ((bf16[64,2,8,512]{3,2,1,0:T(8,128)(2,1)}), bf16[64,2,8,512]{3,2,1,0:T(8,128)(2,1)S(1)}, u32[]{:S(2)}, u32[]{:S(2)}) async-start(bf16[64,2,8,512]{3,2,1,0:T(8,128)(2,1)} %shard_map.91), calls=%async_computation.1 | async-start | bytes 2097152 | tf_op jit(solution)/shard_map/all_to_all | solution.py:244
  74.1 4.2 %shard_map.93 = (f32[2,512,512]{2,1,0:T(8,128)}, f32[2,512,512]{2,1,0:T(8,128)}) custom-call(bf16[64,2,8,512]{3,2,1,0:T(8,128)(2,1)S(1)} %all_to_all.10.held_ref, f32[2,512,512]{2,1,0:T(8,128)} %left_ref.3, f32[2,512,512]{2,1,0:T(8,128)} %right_ref.3), custom_call_target="tpu_custom_call" | custom-call | flops 1073741824 | bytes 10485760 | tf_op jit(solution)/shard_map/pallas_call | solution.py:165
  78.2 24.4 %all-to-all-done.1 = bf16[64,2,8,512]{3,2,1,0:T(8,128)(2,1)S(1)} async-done(((bf16[64,2,8,512]{3,2,1,0:T(8,128)(2,1)}), bf16[64,2,8,512]{3,2,1,0:T(8,128)(2,1)S(1)}, u32[]{:S(2)}, u32[]{:S(2)}) %all-to-all-start.1) | async-done | bytes 1048608 | tf_op jit(solution)/shard_map/all_to_all | solution.py:244
  102.6 1.4 %shard_map.92 = bf16[64,8,512]{2,1,0:T(8,128)(2,1)} custom-call(s32[64]{0:T(128)S(1)} %multiply_add_fusion.place_ref, bf16[128,8,512]{2,1,0:T(8,128)(2,1)S(1)} %bitcast.16), custom_call_target="tpu_custom_call" | custom-call | bytes 2097152 | tf_op jit(solution)/shard_map/pallas_call | solution.py:201
  (4 shorter events, 0.0 us)
Async XLA Ops:
  1.7 11.6 %collective-permute-start.4 = (bf16[32,8,512]{2,1,0:T(8,128)(2,1)S(1)}, bf16[32,8,512]{2,1,0:T(8,128)(2,1)S(1)}, u32[]{:S(2)}, u32[]{:S(2)}) collective-permute-start(bf16[32,8,512]{2,1,0:T(8,128)(2,1)S(1)} %get-tuple-element.21), channel_id=1, source_target_pairs={{0,192},{64,128},{128,64},{192,0},{1,193},{65,129},{129,65},{193,1... | collective-permute-start | bytes 786440 | tf_op jit(solution)/shard_map/ppermute | solution.py:222
  5.4 6.9 %collective-permute-start.2 = (bf16[32,8,512]{2,1,0:T(8,128)(2,1)S(1)}, bf16[32,8,512]{2,1,0:T(8,128)(2,1)S(1)}, u32[]{:S(2)}, u32[]{:S(2)}) collective-permute-start(bf16[32,8,512]{2,1,0:T(8,128)(2,1)S(1)} %get-tuple-element.22), channel_id=1, source_target_pairs={{0,64},{64,0},{128,192},{192,128},{1,65},{65,1},{129,193},{193,129... | collective-permute-start | bytes 786440 | tf_op jit(solution)/shard_map/ppermute | solution.py:222
  5.4 5.1 %copy-start.2 = (s32[256,1]{0,1:T(1,128)S(1)}, s32[256,1]{0,1:T(1,128)}, u32[]{:S(2)}) copy-start(s32[256,1]{0,1:T(1,128)} %param.7) | copy-start | bytes 3076
  7.0 10.8 %collective-permute-start = (bf16[32,8,512]{2,1,0:T(8,128)(2,1)S(1)}, bf16[32,8,512]{2,1,0:T(8,128)(2,1)S(1)}, u32[]{:S(2)}, u32[]{:S(2)}) collective-permute-start(bf16[32,8,512]{2,1,0:T(8,128)(2,1)S(1)} %get-tuple-element.13), channel_id=1, source_target_pairs={{0,64},{64,0},{128,192},{192,128},{1,65},{65,1},{129,193},{193,129... | collective-permute-start | bytes 786440 | tf_op jit(solution)/shard_map/ppermute | solution.py:222
  8.6 9.2 %collective-permute-start.1 = (bf16[32,8,512]{2,1,0:T(8,128)(2,1)S(1)}, bf16[32,8,512]{2,1,0:T(8,128)(2,1)S(1)}, u32[]{:S(2)}, u32[]{:S(2)}) collective-permute-start(bf16[32,8,512]{2,1,0:T(8,128)(2,1)S(1)} %get-tuple-element.14), channel_id=1, source_target_pairs={{0,192},{64,128},{128,64},{192,0},{1,193},{65,129},{129,65},{193,1... | collective-permute-start | bytes 786440 | tf_op jit(solution)/shard_map/ppermute | solution.py:222
  12.3 9.4 %collective-permute-start.3 = (bf16[32,8,512]{2,1,0:T(8,128)(2,1)S(1)}, bf16[32,8,512]{2,1,0:T(8,128)(2,1)S(1)}, u32[]{:S(2)}, u32[]{:S(2)}) collective-permute-start(bf16[32,8,512]{2,1,0:T(8,128)(2,1)S(1)} %shard_map.88), channel_id=1, source_target_pairs={{0,192},{64,128},{128,64},{192,0},{1,193},{65,129},{129,65},{193,1... | collective-permute-start | bytes 786440 | tf_op jit(solution)/shard_map/ppermute | solution.py:222
  13.4 10.0 %collective-permute-start.5 = (bf16[32,8,512]{2,1,0:T(8,128)(2,1)S(1)}, bf16[32,8,512]{2,1,0:T(8,128)(2,1)S(1)}, u32[]{:S(2)}, u32[]{:S(2)}) collective-permute-start(bf16[32,8,512]{2,1,0:T(8,128)(2,1)S(1)} %shard_map.89), channel_id=1, source_target_pairs={{0,64},{64,0},{128,192},{192,128},{1,65},{65,1},{129,193},{193,129... | collective-permute-start | bytes 786440 | tf_op jit(solution)/shard_map/ppermute | solution.py:222
  23.5 42.3 %copy-start = (bf16[2,512,512]{2,1,0:T(8,128)(2,1)S(1)}, bf16[2,512,512]{2,1,0:T(8,128)(2,1)}, u32[]{:S(2)}) copy-start(bf16[2,512,512]{2,1,0:T(8,128)(2,1)} %left_ref.2) | copy-start | bytes 3145732
  23.5 42.3 %copy-start.1 = (bf16[2,512,512]{2,1,0:T(8,128)(2,1)S(1)}, bf16[2,512,512]{2,1,0:T(8,128)(2,1)}, u32[]{:S(2)}) copy-start(bf16[2,512,512]{2,1,0:T(8,128)(2,1)} %right_ref.2) | copy-start | bytes 3145732
  67.8 34.8 %all-to-all-start.1 = ((bf16[64,2,8,512]{3,2,1,0:T(8,128)(2,1)}), bf16[64,2,8,512]{3,2,1,0:T(8,128)(2,1)S(1)}, u32[]{:S(2)}, u32[]{:S(2)}) async-start(bf16[64,2,8,512]{3,2,1,0:T(8,128)(2,1)} %shard_map.91), calls=%async_computation.1 | async-start | bytes 2097152 | tf_op jit(solution)/shard_map/all_to_all | solution.py:244

commit v7 on v6

--- a/solution.py
+++ b/solution.py
@@ -117,12 +117,16 @@
     strips = sems.shape[1]
     height = order // strips
     copies = []
+    halves = []
     for s in range(slot_count):
         block = wide(held_ref[:, s]).reshape(order, order).astype(jnp.bfloat16)
-        half = jnp.dot(left_ref[s], block, preferred_element_type=jnp.float32).astype(jnp.bfloat16)
+        halves.append(
+            jnp.dot(left_ref[s], block, preferred_element_type=jnp.float32).astype(jnp.bfloat16)
+        )
+    for s in range(slot_count):
         for j in range(strips):
             full = jnp.dot(
-                half[j * height : (j + 1) * height], right_ref[s], preferred_element_type=jnp.float32
+                halves[s][j * height : (j + 1) * height], right_ref[s], preferred_element_type=jnp.float32
             )
             run = pl.ds(j * height // rows, height // rows)
             made[s, run] = full.reshape(height // rows, rows, order).astype(jnp.bfloat16)

time: 104 us -> 104 us (level)
  no operation moved by 1% of the time
where the time goes in v7:
time: 104 us
  blocking collectives  41.7 us (40%)
  waiting for transfers between devices  35.5 us (34%)
  starting transfers between devices  12.7 us (12%)
  Pallas kernels  11.8 us (11%)
  local copies, waits for them, and re-layouts  1.16 us (1%)
    all_to_all x1, blocking collectives, on_device(): lax.all_to_all(placed, 'fsdp', split_axis=0, concat_axis=0, tiled=True)  41.7 us
    all_to_all x1, waiting for transfers between devices, on_device(): lax.all_to_all(update_slots, 'fsdp', split_axis=0, concat_axis=0, tiled=T...  24.4 us
    ppermute x6, waiting for transfers between devices, swap(): return lax.ppermute(value, 'rep', [(i, i ^ bit) for i in range(rep_count)])  11.1 us
    ppermute x6, starting transfers between devices, swap(): return lax.ppermute(value, 'rep', [(i, i ^ bit) for i in range(rep_count)])  6.46 us
    all_to_all x1, starting transfers between devices, on_device(): lax.all_to_all(update_slots, 'fsdp', split_axis=0, concat_axis=0, tiled=T...  6.2 us
    pallas_call x1, Pallas kernels, statistics(): pl.pallas_call(stats_kernel, grid=(slot_count,), in_specs=[pl.BlockSpec((...  4.16 us
    pallas_call x2, Pallas kernels, cut(): pl.pallas_call(cut_kernel, in_specs=[IN_SMEM, IN_HBM], out_specs=[IN_VMEM...  3.35 us
  transfers between devices with their start and end apart: 7, of which 5 were waited for; matrix products, arithmetic and copies ran while one was open for 0% of the time, Pallas kernels for 7%

profile of v7, /device:TPU:1, one launch (start us, length us, event | category | flops | bytes accessed | tf_op | source)
XLA Modules:
  0.0 104.0 jit_solution(241259369674790154)
XLA Ops:
  0.6 1.1 %dynamic-slice_bitcast_fusion = (bf16[32,8,512]{2,1,0:T(8,128)(2,1)S(1)}, bf16[32,8,512]{2,1,0:T(8,128)(2,1)S(1)}) fusion(bf16[1,256,8,512]{3,2,1,0:T(8,128)(2,1)} %param.6, s32[]{:T(128)S(6)} %select_n.11, s32[]{:T(128)S(6)} %select_n.10), kind=kLoop, calls=%fused_computation | loop fusion | bytes 1048584 | tf_op jit(solution)/shard_map/dynamic_slice | solution.py:232
  1.7 3.7 %collective-permute-start.4 = (bf16[32,8,512]{2,1,0:T(8,128)(2,1)S(1)}, bf16[32,8,512]{2,1,0:T(8,128)(2,1)S(1)}, u32[]{:S(2)}, u32[]{:S(2)}) collective-permute-start(bf16[32,8,512]{2,1,0:T(8,128)(2,1)S(1)} %get-tuple-element.21), channel_id=1, source_target_pairs={{0,192},{64,128},{128,64},{192,0},{1,193},{65,129},{129,65},{193,1... | collective-permute-start | bytes 786440 | tf_op jit(solution)/shard_map/ppermute | solution.py:226
  5.4 0.0 collective-permute-start.2
  5.4 0.1 pad_add_fusion.1.starts_ref
  5.4 1.6 %shard_map.86 = (bf16[32,8,512]{2,1,0:T(8,128)(2,1)S(1)}, bf16[32,8,512]{2,1,0:T(8,128)(2,1)S(1)}) custom-call(s32[2]{0:T(128)S(1)} %pad_add_fusion.1.starts_ref, bf16[256,8,512]{2,1,0:T(8,128)(2,1)} %bitcast.18), custom_call_target="tpu_custom_call" | custom-call | bytes 2097152 | tf_op jit(solution)/shard_map/pallas_call | solution.py:43
  7.0 1.5 %collective-permute-start = (bf16[32,8,512]{2,1,0:T(8,128)(2,1)S(1)}, bf16[32,8,512]{2,1,0:T(8,128)(2,1)S(1)}, u32[]{:S(2)}, u32[]{:S(2)}) collective-permute-start(bf16[32,8,512]{2,1,0:T(8,128)(2,1)S(1)} %get-tuple-element.13), channel_id=1, source_target_pairs={{0,64},{64,0},{128,192},{192,128},{1,65},{65,1},{129,193},{193,129... | collective-permute-start | bytes 786440 | tf_op jit(solution)/shard_map/ppermute | solution.py:226
  8.6 0.1 collective-permute-start.1
  8.7 0.1 pad_add_fusion.starts_ref
  8.8 1.8 %shard_map.85 = (bf16[64,8,512]{2,1,0:T(8,128)(2,1)S(1)}, bf16[32,8,512]{2,1,0:T(8,128)(2,1)S(1)}, bf16[32,8,512]{2,1,0:T(8,128)(2,1)S(1)}) custom-call(s32[3]{0:T(128)S(1)} %pad_add_fusion.starts_ref, bf16[256,8,512]{2,1,0:T(8,128)(2,1)} %bitcast.19), custom_call_target="tpu_custom_call" | custom-call | bytes 2097152 | tf_op jit(solution)/shard_map/pallas_call | solution.py:43
  10.5 0.0 copy-done.2
  10.5 0.1 fusion.1
  10.6 1.6 %collective-permute-done.2.b_ref = bf16[32,8,512]{2,1,0:T(8,128)(2,1)S(1)} collective-permute-done((bf16[32,8,512]{2,1,0:T(8,128)(2,1)S(1)}, bf16[32,8,512]{2,1,0:T(8,128)(2,1)S(1)}, u32[]{:S(2)}, u32[]{:S(2)}) %collective-permute-start.2) | collective-permute-done | bytes 262176 | tf_op jit(solution)/shard_map/ppermute | solution.py:226
  12.2 0.1 shard_map.88
  12.3 1.1 %collective-permute-start.3 = (bf16[32,8,512]{2,1,0:T(8,128)(2,1)S(1)}, bf16[32,8,512]{2,1,0:T(8,128)(2,1)S(1)}, u32[]{:S(2)}, u32[]{:S(2)}) collective-permute-start(bf16[32,8,512]{2,1,0:T(8,128)(2,1)S(1)} %shard_map.88), channel_id=1, source_target_pairs={{0,192},{64,128},{128,64},{192,0},{1,193},{65,129},{129,65},{193,1... | collective-permute-start | bytes 786440 | tf_op jit(solution)/shard_map/ppermute | solution.py:226
  13.4 0.0 collective-permute-done.4.b_ref
  13.4 0.1 shard_map.89
  13.4 0.1 collective-permute-start.5
  13.5 0.2 convert_reduce_fusion
  13.7 0.1 multiply_add_fusion.place_ref
  13.8 4.1 %collective-permute-done.near_a_ref = bf16[32,8,512]{2,1,0:T(8,128)(2,1)S(1)} collective-permute-done((bf16[32,8,512]{2,1,0:T(8,128)(2,1)S(1)}, bf16[32,8,512]{2,1,0:T(8,128)(2,1)S(1)}, u32[]{:S(2)}, u32[]{:S(2)}) %collective-permute-start) | collective-permute-done | bytes 262176 | tf_op jit(solution)/shard_map/ppermute | solution.py:226
  17.8 0.0 collective-permute-done.1.near_b_ref
  17.8 0.2 shard_map.87
  18.0 3.7 %collective-permute-done.3.far_a_ref = bf16[32,8,512]{2,1,0:T(8,128)(2,1)S(1)} collective-permute-done((bf16[32,8,512]{2,1,0:T(8,128)(2,1)S(1)}, bf16[32,8,512]{2,1,0:T(8,128)(2,1)S(1)}, u32[]{:S(2)}, u32[]{:S(2)}) %collective-permute-start.3) | collective-permute-done | bytes 262176 | tf_op jit(solution)/shard_map/ppermute | solution.py:226
  21.7 1.7 %collective-permute-done.5.far_b_ref = bf16[32,8,512]{2,1,0:T(8,128)(2,1)S(1)} collective-permute-done((bf16[32,8,512]{2,1,0:T(8,128)(2,1)S(1)}, bf16[32,8,512]{2,1,0:T(8,128)(2,1)S(1)}, u32[]{:S(2)}, u32[]{:S(2)}) %collective-permute-start.5) | collective-permute-done | bytes 262176 | tf_op jit(solution)/shard_map/ppermute | solution.py:226
  23.5 0.6 shard_map.90
  24.1 41.7 %all_to_all.10.held_ref = bf16[64,2,8,512]{3,2,1,0:T(8,128)(2,1)S(1)} all-to-all(bf16[64,2,8,512]{3,2,1,0:T(8,128)(2,1)S(1)} %bitcast.17), channel_id=1, replica_groups=mesh['rep'=4,'fsdp'=64] {'fsdp'}, dimensions={0} | all-to-all | bytes 2097152 | tf_op jit(solution)/shard_map/all_to_all | solution.py:246
  65.8 0.0 copy-done.1
  65.8 2.0 %shard_map.91 = bf16[64,2,8,512]{3,2,1,0:T(8,128)(2,1)} custom-call(bf16[64,2,8,512]{3,2,1,0:T(8,128)(2,1)S(1)} %all_to_all.10.held_ref, bf16[2,512,512]{2,1,0:T(8,128)(2,1)S(1)} %copy-done, bf16[2,512,512]{2,1,0:T(8,128)(2,1)S(1)} %copy-done.1), custom_call_target="tpu_custom_call" | custom-call | flops 1073741824 | bytes 4194304 | tf_op jit(solution)/shard_map/pallas_call | solution.py:141
  67.8 6.2 %all-to-all-start.1 = ((bf16[64,2,8,512]{3,2,1,0:T(8,128)(2,1)}), bf16[64,2,8,512]{3,2,1,0:T(8,128)(2,1)S(1)}, u32[]{:S(2)}, u32[]{:S(2)}) async-start(bf16[64,2,8,512]{3,2,1,0:T(8,128)(2,1)} %shard_map.91), calls=%async_computation.1 | async-start | bytes 2097152 | tf_op jit(solution)/shard_map/all_to_all | solution.py:248
  74.1 4.2 %shard_map.93 = (f32[2,512,512]{2,1,0:T(8,128)}, f32[2,512,512]{2,1,0:T(8,128)}) custom-call(bf16[64,2,8,512]{3,2,1,0:T(8,128)(2,1)S(1)} %all_to_all.10.held_ref, f32[2,512,512]{2,1,0:T(8,128)} %left_ref.3, f32[2,512,512]{2,1,0:T(8,128)} %right_ref.3), custom_call_target="tpu_custom_call" | custom-call | flops 1073741824 | bytes 10485760 | tf_op jit(solution)/shard_map/pallas_call | solution.py:169
  78.2 24.4 %all-to-all-done.1 = bf16[64,2,8,512]{3,2,1,0:T(8,128)(2,1)S(1)} async-done(((bf16[64,2,8,512]{3,2,1,0:T(8,128)(2,1)}), bf16[64,2,8,512]{3,2,1,0:T(8,128)(2,1)S(1)}, u32[]{:S(2)}, u32[]{:S(2)}) %all-to-all-start.1) | async-done | bytes 1048608 | tf_op jit(solution)/shard_map/all_to_all | solution.py:248
  102.6 1.4 %shard_map.92 = bf16[64,8,512]{2,1,0:T(8,128)(2,1)} custom-call(s32[64]{0:T(128)S(1)} %multiply_add_fusion.place_ref, bf16[128,8,512]{2,1,0:T(8,128)(2,1)S(1)} %bitcast.16), custom_call_target="tpu_custom_call" | custom-call | bytes 2097152 | tf_op jit(solution)/shard_map/pallas_call | solution.py:205
  (4 shorter events, 0.0 us)
Async XLA Ops:
  1.7 11.6 %collective-permute-start.4 = (bf16[32,8,512]{2,1,0:T(8,128)(2,1)S(1)}, bf16[32,8,512]{2,1,0:T(8,128)(2,1)S(1)}, u32[]{:S(2)}, u32[]{:S(2)}) collective-permute-start(bf16[32,8,512]{2,1,0:T(8,128)(2,1)S(1)} %get-tuple-element.21), channel_id=1, source_target_pairs={{0,192},{64,128},{128,64},{192,0},{1,193},{65,129},{129,65},{193,1... | collective-permute-start | bytes 786440 | tf_op jit(solution)/shard_map/ppermute | solution.py:226
  5.4 6.9 %collective-permute-start.2 = (bf16[32,8,512]{2,1,0:T(8,128)(2,1)S(1)}, bf16[32,8,512]{2,1,0:T(8,128)(2,1)S(1)}, u32[]{:S(2)}, u32[]{:S(2)}) collective-permute-start(bf16[32,8,512]{2,1,0:T(8,128)(2,1)S(1)} %get-tuple-element.22), channel_id=1, source_target_pairs={{0,64},{64,0},{128,192},{192,128},{1,65},{65,1},{129,193},{193,129... | collective-permute-start | bytes 786440 | tf_op jit(solution)/shard_map/ppermute | solution.py:226
  5.4 5.1 %copy-start.2 = (s32[256,1]{0,1:T(1,128)S(1)}, s32[256,1]{0,1:T(1,128)}, u32[]{:S(2)}) copy-start(s32[256,1]{0,1:T(1,128)} %param.7) | copy-start | bytes 3076
  7.0 10.8 %collective-permute-start = (bf16[32,8,512]{2,1,0:T(8,128)(2,1)S(1)}, bf16[32,8,512]{2,1,0:T(8,128)(2,1)S(1)}, u32[]{:S(2)}, u32[]{:S(2)}) collective-permute-start(bf16[32,8,512]{2,1,0:T(8,128)(2,1)S(1)} %get-tuple-element.13), channel_id=1, source_target_pairs={{0,64},{64,0},{128,192},{192,128},{1,65},{65,1},{129,193},{193,129... | collective-permute-start | bytes 786440 | tf_op jit(solution)/shard_map/ppermute | solution.py:226
  8.6 9.2 %collective-permute-start.1 = (bf16[32,8,512]{2,1,0:T(8,128)(2,1)S(1)}, bf16[32,8,512]{2,1,0:T(8,128)(2,1)S(1)}, u32[]{:S(2)}, u32[]{:S(2)}) collective-permute-start(bf16[32,8,512]{2,1,0:T(8,128)(2,1)S(1)} %get-tuple-element.14), channel_id=1, source_target_pairs={{0,192},{64,128},{128,64},{192,0},{1,193},{65,129},{129,65},{193,1... | collective-permute-start | bytes 786440 | tf_op jit(solution)/shard_map/ppermute | solution.py:226
  12.3 9.4 %collective-permute-start.3 = (bf16[32,8,512]{2,1,0:T(8,128)(2,1)S(1)}, bf16[32,8,512]{2,1,0:T(8,128)(2,1)S(1)}, u32[]{:S(2)}, u32[]{:S(2)}) collective-permute-start(bf16[32,8,512]{2,1,0:T(8,128)(2,1)S(1)} %shard_map.88), channel_id=1, source_target_pairs={{0,192},{64,128},{128,64},{192,0},{1,193},{65,129},{129,65},{193,1... | collective-permute-start | bytes 786440 | tf_op jit(solution)/shard_map/ppermute | solution.py:226
  13.4 10.0 %collective-permute-start.5 = (bf16[32,8,512]{2,1,0:T(8,128)(2,1)S(1)}, bf16[32,8,512]{2,1,0:T(8,128)(2,1)S(1)}, u32[]{:S(2)}, u32[]{:S(2)}) collective-permute-start(bf16[32,8,512]{2,1,0:T(8,128)(2,1)S(1)} %shard_map.89), channel_id=1, source_target_pairs={{0,64},{64,0},{128,192},{192,128},{1,65},{65,1},{129,193},{193,129... | collective-permute-start | bytes 786440 | tf_op jit(solution)/shard_map/ppermute | solution.py:226
  23.5 42.3 %copy-start = (bf16[2,512,512]{2,1,0:T(8,128)(2,1)S(1)}, bf16[2,512,512]{2,1,0:T(8,128)(2,1)}, u32[]{:S(2)}) copy-start(bf16[2,512,512]{2,1,0:T(8,128)(2,1)} %left_ref.2) | copy-start | bytes 3145732
  23.5 42.3 %copy-start.1 = (bf16[2,512,512]{2,1,0:T(8,128)(2,1)S(1)}, bf16[2,512,512]{2,1,0:T(8,128)(2,1)}, u32[]{:S(2)}) copy-start(bf16[2,512,512]{2,1,0:T(8,128)(2,1)} %right_ref.2) | copy-start | bytes 3145732
  67.8 34.8 %all-to-all-start.1 = ((bf16[64,2,8,512]{3,2,1,0:T(8,128)(2,1)}), bf16[64,2,8,512]{3,2,1,0:T(8,128)(2,1)S(1)}, u32[]{:S(2)}, u32[]{:S(2)}) async-start(bf16[64,2,8,512]{3,2,1,0:T(8,128)(2,1)} %shard_map.91), calls=%async_computation.1 | async-start | bytes 2097152 | tf_op jit(solution)/shard_map/all_to_all | solution.py:248
